TPU v7x, 512 devices: a whole 4x8x8 slice. The times are simulated.
512 devices in a mesh: gx: 16 (over z, core), gy: 32 (over x, y).
Axes of the slice: x: 4, y: 8, z: 8, core: 2. Of those that a mesh axis runs over, the one named last changes fastest.
Arguments:
- state: float32 [65536, 6, 512], P(('gx', 'gy')), may hold values from -6 to 6
- levels: int32 [65536], P(('gx', 'gy')), may hold values from 0 to 2
- face_source: int32 [393216], P(('gx', 'gy')), may hold values from -1 to 895, as said below
- face_send: int32 [512, 4, 32], P(('gx', 'gy')), may hold values from 0 to 767, as said below
- mort_owner: int32 [512, 32, 1], P(('gx', 'gy')), may hold values from -1 to 767, as said below
- mort_child: int32 [512, 32, 4], P(('gx', 'gy')), may hold values from -1 to 767, as said below
- flux_jac: float32 [3, 6, 6], replicated, may hold values from -1.75 to 1.75
- penalty: float32 [6], replicated, may hold values from 0.5 to 1.5
Outputs:
- increment: float32 [65536, 6, 512], P(('gx', 'gy'))
Inputs may be any that keep to these rules, and one draw needn't show every extreme that they name: `face_source`: values 0 to 767 name a face of the same device (a face naming itself has no jump); 768 + o * 32 + c names slot c of arrived block o; -1 marks a face on a mortar. Faces paired across devices see each other. `face_send`: local face slots, all distinct on one device, none on a mortar. `mort_owner`: entry [y', k] of device (x, y) is its large face whose four children lie on device (x, y') at slots 4 k to 4 k + 3 of that device's mort_child row y, quadrant = slot modulo 4; -1 where unused. Every device owns one mortar whose children lie on the next device along gy, wrapping; any other pair of devices with the same gx index, a device with itself included, may share a mortar or not, and owners differ in how many they hold. `mort_child`: entry [y, j] of a device is its face on quadrant j modulo 4 of mortar j // 4 owned by device y of the same gx index; -1 where unused, in whole groups of four.
All inputs are finite; a program needn't handle non-finite values.
Results may differ from a plain program's by a relative error of at most 0.0003.
Values sent between devices are 32-bit elements; how exact they have to be, the bound alone decides.
No kernel may reach another device: no remote copies, remote signals or barrier semaphores. Data moves between devices by JAX's collectives and lax.ppermute only.
A program may use at most 64 MiB of HBM per device.

v0:
```python
import jax
import jax.numpy as jnp
import numpy as np
from jax import lax
from jax.sharding import PartitionSpec as P

P_SIZE = 7


OFFSETS = (-2, -1, 1, 2)
step_size = 0.01


def shifted(value, axis, steps):
    count = lax.axis_size(axis)
    pairs = [(source, (source + steps) % count) for source in range(count)]
    return lax.ppermute(value, axis, pairs)


def basis_tables(order):
    per_dim = order + 1
    eye_small = np.eye(per_dim)
    points = -np.cos(np.pi * np.arange(per_dim) / order)
    differences = points[:, None] - points[None, :] + eye_small
    barycentric = 1.0 / np.prod(differences, axis=1)
    derivative = barycentric[None, :] / barycentric[:, None] / differences
    derivative = np.where(eye_small > 0, 0.0, derivative)
    derivative = derivative - eye_small * derivative.sum(axis=1)[:, None]
    angles = np.pi * np.arange(per_dim) / order
    weights = np.ones(per_dim)
    for wave in range(1, order // 2 + 1):
        factor = 2.0
        weights = weights - factor * np.cos(2.0 * wave * angles) / (4.0 * wave * wave - 1.0)
    edge_factor = np.where((np.arange(per_dim) == 0) | (np.arange(per_dim) == order), 1.0, 2.0)
    weights = edge_factor * weights / order

    def lagrange(targets):
        values_at = np.ones((per_dim, per_dim))
        for column in range(per_dim):
            for other in range(per_dim):
                if other != column:
                    values_at[:, column] *= (targets - points[other]) / (
                        points[column] - points[other]
                    )
        return values_at

    halves = [lagrange((points - 1.0) / 2.0), lagrange((points + 1.0) / 2.0)]
    identity = np.eye(per_dim)
    deriv_mats = np.stack(
        [
            np.kron(np.kron(derivative, identity), identity).T,
            np.kron(np.kron(identity, derivative), identity).T,
            np.kron(np.kron(identity, identity), derivative).T,
        ]
    )
    node_index = np.arange(per_dim**3).reshape(per_dim, per_dim, per_dim)
    fnodes = per_dim * per_dim
    select = np.zeros((per_dim**3, 6 * fnodes))
    for face in range(6):
        ending = 0 if face % 2 == 0 else order
        picker = [slice(None), slice(None), slice(None)]
        picker[face // 2] = ending
        on_face = node_index[tuple(picker)].reshape(-1)
        select[on_face, face * fnodes + np.arange(fnodes)] = 1.0
    lift_mat = select.T / weights[0]
    face_weight = np.kron(weights, weights)
    proj = np.stack([np.kron(halves[quad // 2], halves[quad % 2]) for quad in range(4)])
    restrict = np.stack(
        [0.25 * (proj[quad].T * face_weight[None, :]) / face_weight[:, None] for quad in range(4)]
    )
    return (
        jnp.asarray(deriv_mats, jnp.float32),
        jnp.asarray(select, jnp.float32),
        jnp.asarray(lift_mat, jnp.float32),
        jnp.asarray(proj, jnp.float32),
        jnp.asarray(restrict, jnp.float32),
    )


def project(large, proj):
    peers, pairs, width = large.shape
    fnodes = proj.shape[1]
    parts = large.reshape(peers, pairs, width // fnodes, fnodes)
    onto = jnp.einsum("pkfm,qnm->pkqfn", parts, proj, precision=lax.Precision.HIGHEST)
    return onto.reshape(peers, pairs * 4, width)


def restrict_sum(jumps, restrict):
    peers, quads, width = jumps.shape
    fnodes = restrict.shape[1]
    parts = jumps.reshape(peers, quads // 4, 4, width // fnodes, fnodes)
    back = jnp.einsum("pkqfn,qmn->pkfm", parts, restrict, precision=lax.Precision.HIGHEST)
    return -back.reshape(peers, quads // 4, width)


def add_rows(jump, index, values):
    target = jnp.where(index < 0, jump.shape[0], index)
    return jump.at[target].add(values, mode="drop")


def rows_masked(traces, index):
    return jnp.where(index[:, None] >= 0, traces[jnp.maximum(index, 0)], 0.0)


def element_rhs(block, level_block, jump, deriv_mats, lift_mat, flux_jac, penalty):
    highest = lax.Precision.HIGHEST
    elements, fields, per_node = block.shape
    fnodes = lift_mat.shape[0] // 6
    flat = block.reshape(elements * fields, per_node)
    grads = jnp.stack(
        [jnp.dot(flat, deriv_mats[direction], precision=highest) for direction in range(3)]
    )
    grads = grads.reshape(3, elements, fields, per_node)
    volume = jnp.einsum("dgh,dehn->egn", flux_jac, grads, precision=highest)
    signs = jnp.array([-1.0, 1.0, -1.0, 1.0, -1.0, 1.0], jnp.float32)
    normal_jac = signs[:, None, None] * jnp.repeat(flux_jac, 2, axis=0)
    faces = jump.reshape(elements, 6, fields, fnodes)
    surface = 0.5 * (
        jnp.einsum("tgh,ethn->etgn", normal_jac, faces, precision=highest)
        - penalty[None, None, :, None] * faces
    )
    lifted = jnp.dot(
        surface.transpose(0, 2, 1, 3).reshape(elements * fields, 6 * fnodes),
        lift_mat,
        precision=highest,
    )
    lifted = lifted.reshape(elements, fields, per_node)
    scale = jnp.exp2(level_block.astype(jnp.float32))
    return step_size * scale[:, None, None] * (lifted - volume)


def per_device(state, levels, face_source, face_send, mort_owner, mort_child, flux_jac, penalty):
    deriv_mats, select, lift_mat, proj, restrict = basis_tables(P_SIZE)
    highest = lax.Precision.HIGHEST
    elements, fields, per_node = state.shape
    fnodes = lift_mat.shape[0] // 6
    slots = 6 * elements
    width = fields * fnodes
    values = jnp.dot(state.reshape(elements * fields, per_node), select, precision=highest)
    traces = values.reshape(elements, fields, 6, fnodes).transpose(0, 2, 1, 3).reshape(slots, width)
    send_rows = face_send.reshape(4, -1)
    arrived = []
    for place in range(4):
        outgoing = traces[send_rows[place]]
        arrived.append(shifted(outgoing, ("gx", "gy"), OFFSETS[place]))
    table_all = jnp.concatenate([traces] + arrived, axis=0)
    neighbour = table_all[jnp.maximum(face_source, 0)]
    jump = jnp.where(face_source[:, None] >= 0, traces - neighbour, 0.0)
    peers = lax.axis_size("gy")
    owner_idx = mort_owner.reshape(-1)
    child_idx = mort_child.reshape(-1)
    large = rows_masked(traces, owner_idx).reshape(peers, -1, width)
    small = rows_masked(traces, child_idx).reshape(peers, -1, width)
    got_small = lax.all_to_all(small, "gy", split_axis=0, concat_axis=0, tiled=True)
    owner_jump = got_small - project(large, proj)
    owner_add = restrict_sum(owner_jump, restrict)
    child_add = lax.all_to_all(owner_jump, "gy", split_axis=0, concat_axis=0, tiled=True)
    jump = add_rows(jump, child_idx, child_add.reshape(-1, width))
    jump = add_rows(jump, owner_idx, owner_add.reshape(-1, width))
    return element_rhs(state, levels, jump, deriv_mats, lift_mat, flux_jac, penalty)


def solution(mesh):
    in_specs = (
        P(("gx", "gy"), None, None),
        P(("gx", "gy")),
        P(("gx", "gy")),
        P(("gx", "gy"), None, None),
        P(("gx", "gy"), None, None),
        P(("gx", "gy"), None, None),
        P(),
        P(),
    )
    out_specs = P(("gx", "gy"), None, None)
    return jax.shard_map(
        per_device, mesh=mesh, in_specs=in_specs, out_specs=out_specs, check_vma=False
    )
```

profile of v0, /device:TPU:8, one launch (start us, length us, event | category | flops | bytes accessed | tf_op | source)
XLA Modules:
  0.0 120.9 jit_solution(4024729863175766994)
XLA Ops:
  1.4 3.2 %fusion.4 = f32[128,6,6,64]{0,3,2,1:T(8,128)S(1)} fusion(f32[6,64,512,1]{2,1,3,0:T(8,128)} %constant.55, f32[128,6,512]{2,0,1:T(8,128)S(1)} %copy-done), kind=kOutput, calls=%fused_computation.20 | convolution fusion | flops 1811939328 | bytes 3538944 | tf_op jit(solution)/shard_map/dot_general | solution.py:139
  4.6 2.3 %copy.34 = f32[128,6,6,64]{3,2,1,0:T(8,128)} copy(f32[128,6,6,64]{0,3,2,1:T(8,128)S(1)} %fusion.4) | data formatting | bytes 2359296 | tf_op jit(solution)/shard_map/transpose | solution.py:140
  6.9 2.7 %reshape.305 = f32[768,384]{1,0:T(8,128)S(1)} reshape(f32[128,6,6,64]{3,2,1,0:T(8,128)} %copy.34) | data formatting | bytes 2359296 | tf_op jit(solution)/shard_map/reshape | solution.py:140
  10.9 15.4 %collective-permute-start = (f32[32,384]{1,0:T(8,128)}, f32[32,384]{1,0:T(8,128)}, u32[]{:S(2)}, u32[]{:S(2)}) collective-permute-start(f32[32,384]{1,0:T(8,128)} %gather_fusion), channel_id=1, source_target_pairs={{0,510},{1,511},{2,0},{3,1},{4,2},{5,3},{6,4},{7,5},{8,6},{9,7},{1... | collective-permute-start | bytes 147464 | tf_op jit(solution)/shard_map/ppermute | solution.py:17
  27.5 3.2 %collective-permute-start.1 = (f32[32,384]{1,0:T(8,128)}, f32[32,384]{1,0:T(8,128)}, u32[]{:S(2)}, u32[]{:S(2)}) collective-permute-start(f32[32,384]{1,0:T(8,128)} %gather_fusion.1), channel_id=1, source_target_pairs={{0,511},{1,0},{2,1},{3,2},{4,3},{5,4},{6,5},{7,6},{8,7},{9,8},{10,... | collective-permute-start | bytes 147464 | tf_op jit(solution)/shard_map/ppermute | solution.py:17
  32.0 2.6 %collective-permute-start.2 = (f32[32,384]{1,0:T(8,128)}, f32[32,384]{1,0:T(8,128)}, u32[]{:S(2)}, u32[]{:S(2)}) collective-permute-start(f32[32,384]{1,0:T(8,128)} %gather_fusion.2), channel_id=1, source_target_pairs={{0,1},{1,2},{2,3},{3,4},{4,5},{5,6},{6,7},{7,8},{8,9},{9,10},{10,1... | collective-permute-start | bytes 147464 | tf_op jit(solution)/shard_map/ppermute | solution.py:17
  35.8 1.9 %collective-permute-start.3 = (f32[32,384]{1,0:T(8,128)}, f32[32,384]{1,0:T(8,128)}, u32[]{:S(2)}, u32[]{:S(2)}) collective-permute-start(f32[32,384]{1,0:T(8,128)} %gather_fusion.3), channel_id=1, source_target_pairs={{0,2},{1,3},{2,4},{3,5},{4,6},{5,7},{6,8},{7,9},{8,10},{9,11},{10,... | collective-permute-start | bytes 147464 | tf_op jit(solution)/shard_map/ppermute | solution.py:17
  39.7 5.6 %all-to-all-start = ((f32[32,4,384]{2,1,0:T(4,128)}), f32[32,4,384]{2,1,0:T(4,128)}, u32[]{:S(2)}, u32[]{:S(2)}) async-start(f32[32,4,384]{2,1,0:T(4,128)} %broadcast_select_fusion), calls=%async_computation | async-start | bytes 393216 | tf_op jit(solution)/shard_map/all_to_all | solution.py:154
  46.8 4.0 %convolution_bitcast_fusion.1 = f32[1,128,6,512]{1,3,2,0:T(8,128)S(1)} fusion(f32[512,512,1]{0,1,2:T(8,128)} %constant.61, f32[128,6,512]{2,0,1:T(8,128)S(1)} %copy-done), kind=kOutput, calls=%fused_computation.17 | convolution fusion | flops 2415919104 | bytes 4194304 | tf_op jit(solution)/shard_map/dot_general | solution.py:111
  50.8 2.7 %convolution_bitcast_fusion.2 = f32[1,128,6,512]{1,3,2,0:T(8,128)S(1)} fusion(f32[512,512,1]{0,1,2:T(8,128)S(1)} %copy-done.6, f32[128,6,512]{2,0,1:T(8,128)S(1)} %copy-done), kind=kOutput, calls=%fused_computation.18 | convolution fusion | flops 2415919104 | bytes 4194304 | tf_op jit(solution)/shard_map/dot_general | solution.py:111
  53.6 2.7 %convolution_bitcast_fusion.3 = f32[1,128,6,512]{1,3,2,0:T(8,128)S(1)} fusion(f32[512,512,1]{0,1,2:T(8,128)S(1)} %copy-done.5, f32[128,6,512]{2,0,1:T(8,128)S(1)} %copy-done), kind=kOutput, calls=%fused_computation.19 | convolution fusion | flops 2415919104 | bytes 4194304 | tf_op jit(solution)/shard_map/dot_general | solution.py:111
  56.3 2.7 %pad_maximum_fusion = f32[3,128,6,512]{1,3,2,0:T(8,128)} fusion(f32[1,128,6,512]{1,3,2,0:T(8,128)S(1)} %convolution_bitcast_fusion.1, f32[1,128,6,512]{1,3,2,0:T(8,128)S(1)} %convolution_bitcast_fusion.2, f32[1,128,6,512]{1,3,2,0:T(8,128)S(1)} %convolution_bitcast_fusion.3), kind=kLoop, calls=%fused_computation.9 | loop fusion | flops 2359296 | bytes 9437184 | tf_op jit(solution)/shard_map/stack | solution.py:110
  59.0 6.3 %copy.46 = f32[3,128,6,512]{3,2,0,1:T(8,128)} copy(f32[3,128,6,512]{1,3,2,0:T(8,128)} %pad_maximum_fusion) | data formatting | bytes 9437184 | tf_op jit(solution)/shard_map/stack | solution.py:110
  65.3 1.9 %gather_fusion.6 = f32[32,384]{1,0:T(8,128)S(1)} fusion(f32[768,384]{1,0:T(8,128)} %copy-done.1, s32[1024]{0:T(1024)S(1)} %get-tuple-element.13), kind=kCustom, calls=%fused_computation.6 | custom fusion | bytes 98432 | tf_op jit(solution)/shard_map/gather | solution.py:102
  67.3 8.0 %convolution_bitcast_fusion = f32[128,512,6]{1,2,0:T(8,128)} fusion(f32[3,128,6,512]{3,2,0,1:T(8,128)} %copy.46, f32[3,6,6]{2,1,0:T(8,128)S(1)} %copy-done.10), kind=kOutput, calls=%fused_computation.10 | convolution fusion | flops 84934656 | bytes 6291888 | tf_op jit(solution)/shard_map/dgh,dehn->egn/dot_general | solution.py:114
  80.3 3.0 %gather_fusion.4 = f32[768,384]{1,0:T(8,128)} fusion(f32[896,384]{1,0:T(8,128)S(1)} %constant_dynamic-update-slice_fusion, s32[1024]{0:T(1024)S(1)} %pad_clamp_fusion.2), kind=kCustom, calls=%fused_computation.4 | custom fusion | bytes 2362368 | tf_op jit(solution)/shard_map/gather | solution.py:147
  85.2 9.9 %all-to-all-start.1 = ((f32[32,4,384]{2,1,0:T(4,128)}), f32[32,4,384]{2,1,0:T(4,128)}, u32[]{:S(2)}, u32[]{:S(2)}) async-start(f32[32,4,384]{2,1,0:T(4,128)} %copy.40), calls=%async_computation.1 | async-start | bytes 393216 | tf_op jit(solution)/shard_map/all_to_all | solution.py:157
  95.2 2.5 %subtract_select_fusion = f32[768,384]{1,0:T(8,128)} fusion(f32[768,384]{1,0:T(8,128)S(1)} %copy-done.2, f32[768,384]{1,0:T(8,128)} %gather_fusion.4, pred[768]{0:T(1024)(128)(4,1)S(1)} %broadcast_compare_fusion), kind=kLoop, calls=%fused_computation.23 | loop fusion | flops 589824 | bytes 3539712 | tf_op jit(solution)/shard_map/jit(_where)/select_n | solution.py:148
  99.4 6.3 %all-to-all-done.1 = f32[32,4,384]{2,1,0:T(4,128)} async-done(((f32[32,4,384]{2,1,0:T(4,128)}), f32[32,4,384]{2,1,0:T(4,128)}, u32[]{:S(2)}, u32[]{:S(2)}) %all-to-all-start.1) | async-done | bytes 196640 | tf_op jit(solution)/shard_map/all_to_all | solution.py:157
  106.7 1.8 %scatter_fusion = f32[768,384]{1,0:T(8,128)S(1)} fusion(f32[768,384]{1,0:T(8,128)S(1)} %copy-done.3, s32[128]{0:T(128)S(1)} %get-tuple-element.12, f32[128,384]{1,0:T(8,128)S(1)} %reshape.372), kind=kCustom, calls=%fused_computation.7 | custom fusion | flops 49152 | bytes 590336 | tf_op jit(solution)/shard_map/scatter-add | solution.py:98
  109.8 2.2 %reshape.310 = f32[128,6,6,64]{3,2,1,0:T(8,128)} reshape(f32[768,384]{1,0:T(8,128)S(1)} %scatter_fusion.1) | data formatting | bytes 2359296 | tf_op jit(solution)/shard_map/reshape | solution.py:117
  112.0 2.5 %copy.43 = f32[128,6,6,64]{0,2,3,1:T(8,128)S(1)} copy(f32[128,6,6,64]{3,2,1,0:T(8,128)} %reshape.310) | data formatting | bytes 2359296 | tf_op jit(solution)/shard_map/reshape | solution.py:117
  114.5 1.5 %fusion.1 = f32[128,6,6,64]{0,2,3,1:T(8,128)S(1)} fusion(f32[128,6,6,64]{0,2,3,1:T(8,128)S(1)} %copy.43, f32[6]{0:T(128)S(1)} %copy-done.15, f32[6,6,6]{2,1,0:T(8,128)S(1)} %bitcast_multiply_fusion), kind=kOutput, calls=%fused_computation.14 | convolution fusion | flops 22118400 | bytes 2360184 | tf_op jit(solution)/shard_map/tgh,ethn->etgn/dot_general | solution.py:119
  116.2 4.6 %fusion = f32[128,6,512]{2,0,1:T(8,128)} fusion(f32[128,512,6]{1,2,0:T(8,128)S(1)} %copy-done.4, f32[384,512,1]{1,0,2:T(8,128)S(1)} %copy-done.8, f32[128,6,384]{0,1,2:T(8,128)S(1)} %bitcast.115, f32[128]{0:T(128)S(1)} %exponential_multiply_fusion), kind=kOutput, calls=%fused_computation.12 | convolution fusion | flops 1812725760 | bytes 5112320 | tf_op jit(solution)/shard_map/dot_general | solution.py:122
  (84 shorter events, 20.7 us)
Async XLA Ops:
  0.0 1.4 %copy-start = (f32[128,6,512]{2,0,1:T(8,128)S(1)}, f32[128,6,512]{2,0,1:T(8,128)}, u32[]{:S(2)}) copy-start(f32[128,6,512]{2,0,1:T(8,128)} %param.14) | copy-start | bytes 4718596
  6.9 2.7 %copy-start.13 = (s32[1,4,32]{2,1,0:T(4,128)S(1)}, s32[1,4,32]{2,1,0:T(4,128)}, u32[]{:S(2)}) copy-start(s32[1,4,32]{2,1,0:T(4,128)} %param.17) | copy-start | bytes 1540
  9.7 29.1 %copy-start.1 = (f32[768,384]{1,0:T(8,128)}, f32[768,384]{1,0:T(8,128)S(1)}, u32[]{:S(2)}) copy-start(f32[768,384]{1,0:T(8,128)S(1)} %reshape.305) | copy-start | bytes 3538948
  9.7 28.1 %copy-start.12 = (s32[1,32,4]{1,2,0:T(4,128)S(1)}, s32[1,32,4]{1,2,0:T(4,128)}, u32[]{:S(2)}) copy-start(s32[1,32,4]{1,2,0:T(4,128)} %param.19) | copy-start | bytes 1540
  9.7 28.3 %copy-start.16 = (s32[1,32,1]{1,2,0:T(1,128)S(1)}, s32[1,32,1]{1,2,0:T(1,128)}, u32[]{:S(2)}) copy-start(s32[1,32,1]{1,2,0:T(1,128)} %param.18) | copy-start | bytes 388
  10.9 66.1 %collective-permute-start = (f32[32,384]{1,0:T(8,128)}, f32[32,384]{1,0:T(8,128)}, u32[]{:S(2)}, u32[]{:S(2)}) collective-permute-start(f32[32,384]{1,0:T(8,128)} %gather_fusion), channel_id=1, source_target_pairs={{0,510},{1,511},{2,0},{3,1},{4,2},{5,3},{6,4},{7,5},{8,6},{9,7},{1... | collective-permute-start | bytes 147464 | tf_op jit(solution)/shard_map/ppermute | solution.py:17
  27.5 50.3 %collective-permute-start.1 = (f32[32,384]{1,0:T(8,128)}, f32[32,384]{1,0:T(8,128)}, u32[]{:S(2)}, u32[]{:S(2)}) collective-permute-start(f32[32,384]{1,0:T(8,128)} %gather_fusion.1), channel_id=1, source_target_pairs={{0,511},{1,0},{2,1},{3,2},{4,3},{5,4},{6,5},{7,6},{8,7},{9,8},{10,... | collective-permute-start | bytes 147464 | tf_op jit(solution)/shard_map/ppermute | solution.py:17
  32.0 46.7 %collective-permute-start.2 = (f32[32,384]{1,0:T(8,128)}, f32[32,384]{1,0:T(8,128)}, u32[]{:S(2)}, u32[]{:S(2)}) collective-permute-start(f32[32,384]{1,0:T(8,128)} %gather_fusion.2), channel_id=1, source_target_pairs={{0,1},{1,2},{2,3},{3,4},{4,5},{5,6},{6,7},{7,8},{8,9},{9,10},{10,1... | collective-permute-start | bytes 147464 | tf_op jit(solution)/shard_map/ppermute | solution.py:17
  35.8 43.7 %collective-permute-start.3 = (f32[32,384]{1,0:T(8,128)}, f32[32,384]{1,0:T(8,128)}, u32[]{:S(2)}, u32[]{:S(2)}) collective-permute-start(f32[32,384]{1,0:T(8,128)} %gather_fusion.3), channel_id=1, source_target_pairs={{0,2},{1,3},{2,4},{3,5},{4,6},{5,7},{6,8},{7,9},{8,10},{9,11},{10,... | collective-permute-start | bytes 147464 | tf_op jit(solution)/shard_map/ppermute | solution.py:17
  38.9 7.8 %copy-start.11 = (s32[768]{0:T(1024)S(1)}, s32[768]{0:T(1024)}, u32[]{:S(2)}) copy-start(s32[768]{0:T(1024)} %param.16) | copy-start | bytes 9220
  39.7 43.6 %all-to-all-start = ((f32[32,4,384]{2,1,0:T(4,128)}), f32[32,4,384]{2,1,0:T(4,128)}, u32[]{:S(2)}, u32[]{:S(2)}) async-start(f32[32,4,384]{2,1,0:T(4,128)} %broadcast_select_fusion), calls=%async_computation | async-start | bytes 393216 | tf_op jit(solution)/shard_map/all_to_all | solution.py:154
  46.8 4.1 %copy-start.6 = (f32[512,512,1]{0,1,2:T(8,128)S(1)}, f32[512,512,1]{0,1,2:T(8,128)}, u32[]{:S(2)}) copy-start(f32[512,512,1]{0,1,2:T(8,128)} %constant.60) | copy-start | bytes 3145732
  50.8 2.7 %copy-start.5 = (f32[512,512,1]{0,1,2:T(8,128)S(1)}, f32[512,512,1]{0,1,2:T(8,128)}, u32[]{:S(2)}) copy-start(f32[512,512,1]{0,1,2:T(8,128)} %constant.59) | copy-start | bytes 3145732
  59.0 8.3 %copy-start.17 = (s32[128]{0:T(128)S(1)}, s32[128]{0:T(128)}, u32[]{:S(2)}) copy-start(s32[128]{0:T(128)} %param.15) | copy-start | bytes 1540
  59.0 8.3 %copy-start.10 = (f32[3,6,6]{2,1,0:T(8,128)S(1)}, f32[3,6,6]{2,1,0:T(8,128)}, u32[]{:S(2)}) copy-start(f32[3,6,6]{2,1,0:T(8,128)} %param.20) | copy-start | bytes 1300
  67.3 8.1 %copy-start.9 = (f32[4,64,64,1]{2,1,3,0:T(8,128)S(1)}, f32[4,64,64,1]{2,1,3,0:T(8,128)}, u32[]{:S(2)}) copy-start(f32[4,64,64,1]{2,1,3,0:T(8,128)} %constant.56) | copy-start | bytes 196612
  75.3 1.7 %copy-start.14 = (f32[6]{0:T(128)S(1)}, f32[6]{0:T(128)}, u32[]{:S(2)}) copy-start(f32[6]{0:T(128)} %constant.40.clone) | copy-start | bytes 76
  80.3 3.0 %copy-start.7 = (f32[32,4,384]{2,0,1:T(8,128)S(1)}, f32[32,4,384]{2,0,1:T(8,128)}, u32[]{:S(2)}) copy-start(f32[32,4,384]{2,0,1:T(8,128)} %reshape.307) | copy-start | bytes 589828
  83.3 11.8 %copy-start.2 = (f32[768,384]{1,0:T(8,128)S(1)}, f32[768,384]{1,0:T(8,128)}, u32[]{:S(2)}) copy-start(f32[768,384]{1,0:T(8,128)} %copy-done.1) | copy-start | bytes 3538948
  85.2 20.5 %all-to-all-start.1 = ((f32[32,4,384]{2,1,0:T(4,128)}), f32[32,4,384]{2,1,0:T(4,128)}, u32[]{:S(2)}, u32[]{:S(2)}) async-start(f32[32,4,384]{2,1,0:T(4,128)} %copy.40), calls=%async_computation.1 | async-start | bytes 393216 | tf_op jit(solution)/shard_map/all_to_all | solution.py:157
  97.6 9.1 %copy-start.3 = (f32[768,384]{1,0:T(8,128)S(1)}, f32[768,384]{1,0:T(8,128)}, u32[]{:S(2)}) copy-start(f32[768,384]{1,0:T(8,128)} %subtract_select_fusion) | copy-start | bytes 3538948
  112.0 2.5 %copy-start.15 = (f32[6]{0:T(128)S(1)}, f32[6]{0:T(128)}, u32[]{:S(2)}) copy-start(f32[6]{0:T(128)} %param.21) | copy-start | bytes 76
  114.5 1.6 %copy-start.4 = (f32[128,512,6]{1,2,0:T(8,128)S(1)}, f32[128,512,6]{1,2,0:T(8,128)}, u32[]{:S(2)}) copy-start(f32[128,512,6]{1,2,0:T(8,128)} %convolution_bitcast_fusion) | copy-start | bytes 4718596
  114.5 1.8 %copy-start.8 = (f32[384,512,1]{1,0,2:T(8,128)S(1)}, f32[384,512,1]{1,0,2:T(8,128)}, u32[]{:S(2)}) copy-start(f32[384,512,1]{1,0,2:T(8,128)} %constant.58) | copy-start | bytes 2359300
where the time goes:
time: 122 us; the launch traced here: 121 us
  starting transfers between devices  38.7 us (32%)
  local copies, waits for them, and re-layouts  36.4 us (30%)
  matrix products  28.8 us (24%)
  other arithmetic  10.2 us (8%)
  waiting for transfers between devices  6.35 us (5%)
    ppermute x4, starting transfers between devices, shifted(): return lax.ppermute(value, axis, pairs)  23.1 us
    all_to_all x1, starting transfers between devices, per_device(): lax.all_to_all(owner_jump, 'gy', split_axis=0, concat_axis=0, tiled=True)  9.94 us
    dot_general x3, matrix products, element_rhs(): jnp.dot(flat, deriv_mats[direction], precision=highest)  9.48 us
    dot_general x1, matrix products, element_rhs(): volume = jnp.einsum('dgh,dehn->egn', flux_jac, grads, precision=highest)  7.96 us
    all_to_all x1, waiting for transfers between devices, per_device(): lax.all_to_all(owner_jump, 'gy', split_axis=0, concat_axis=0, tiled=True)  6.34 us
    another operation x1, local copies, waits for them, and re-layouts, element_rhs(): jnp.stack([jnp.dot(flat, deriv_mats[direction], precision=highest) for di...  6.3 us
    all_to_all x1, starting transfers between devices, per_device(): lax.all_to_all(small, 'gy', split_axis=0, concat_axis=0, tiled=True)  5.63 us
    unnamed x41, local copies, waits for them, and re-layouts  5.53 us
  transfers between devices with their start and end apart: 6, of which 1 were waited for; matrix products, arithmetic and copies ran while one was open for 39% of the time, Pallas kernels for 0%

commit v1 on v0

v1 whole, which is shorter than its diff:
```python
import jax
import jax.numpy as jnp
import ml_dtypes
import numpy as np
from jax import lax
from jax.experimental import pallas as pl
from jax.experimental.pallas import tpu as pltpu
from jax.sharding import PartitionSpec as P

P_SIZE = 7
OFFSETS = (-2, -1, 1, 2)
STEP_SIZE = 0.01

F32 = jnp.float32
BF16 = jnp.bfloat16
HIGHEST = lax.Precision.HIGHEST
VMEM = pl.BlockSpec(memory_space=pltpu.VMEM)
SMEM = pl.BlockSpec(memory_space=pltpu.SMEM)
MIB = 1 << 20


def shifted(value, axis, steps):
    count = lax.axis_size(axis)
    pairs = [(source, (source + steps) % count) for source in range(count)]
    return lax.ppermute(value, axis, pairs)


def pieces_of(table):
    rest = np.asarray(table, np.float32)
    out = []
    for _ in range(3):
        piece = rest.astype(ml_dtypes.bfloat16)
        out.append(piece)
        rest = rest - piece.astype(np.float32)
    return np.stack(out)


def basis_tables(order):
    per_dim = order + 1
    eye_small = np.eye(per_dim)
    points = -np.cos(np.pi * np.arange(per_dim) / order)
    differences = points[:, None] - points[None, :] + eye_small
    barycentric = 1.0 / np.prod(differences, axis=1)
    derivative = barycentric[None, :] / barycentric[:, None] / differences
    derivative = np.where(eye_small > 0, 0.0, derivative)
    derivative = derivative - eye_small * derivative.sum(axis=1)[:, None]
    angles = np.pi * np.arange(per_dim) / order
    weights = np.ones(per_dim)
    for wave in range(1, order // 2 + 1):
        factor = 1.0 if 2 * wave == order else 2.0
        weights = weights - factor * np.cos(2.0 * wave * angles) / (4.0 * wave * wave - 1.0)
    edge_factor = np.where((np.arange(per_dim) == 0) | (np.arange(per_dim) == order), 1.0, 2.0)
    weights = edge_factor * weights / order

    def lagrange(targets):
        values_at = np.ones((per_dim, per_dim))
        for column in range(per_dim):
            for other in range(per_dim):
                if other != column:
                    values_at[:, column] *= (targets - points[other]) / (
                        points[column] - points[other]
                    )
        return values_at

    halves = [lagrange((points - 1.0) / 2.0), lagrange((points + 1.0) / 2.0)]
    identity = np.eye(per_dim)
    node_index = np.arange(per_dim**3).reshape(per_dim, per_dim, per_dim)
    fnodes = per_dim * per_dim
    select = np.zeros((per_dim**3, 4 * fnodes), np.float32)
    for face in range(2, 6):
        picker = [slice(None), slice(None), slice(None)]
        picker[face // 2] = 0 if face % 2 == 0 else order
        on_face = node_index[tuple(picker)].reshape(-1)
        select[on_face, (face - 2) * fnodes + np.arange(fnodes)] = 1.0
    face_weight = np.kron(weights, weights)
    proj = [np.kron(halves[quad // 2], halves[quad % 2]) for quad in range(4)]
    restrict = [
        0.25 * (proj[quad].T * face_weight[None, :]) / face_weight[:, None] for quad in range(4)
    ]
    two = np.eye(2)
    both = sum(restrict[quad] @ proj[quad] for quad in range(4))
    quarter = np.eye(4)
    return {
        "select": select.astype(ml_dtypes.bfloat16),
        "lift": np.ascontiguousarray(select.T).astype(ml_dtypes.bfloat16),
        "restrict": np.concatenate([np.kron(two, r.T) for r in restrict], 0).astype(np.float32),
        "project": np.concatenate([np.kron(two, p.T) for p in proj], 1).astype(np.float32),
        "both": np.kron(two, both.T).astype(np.float32),
        "deriv_0": pieces_of(np.kron(derivative, np.eye(fnodes)).T),
        "deriv_1": pieces_of(np.kron(quarter, np.kron(derivative, identity)).T),
        "deriv_2": pieces_of(np.kron(quarter, np.kron(identity, derivative)).T),
        "edge": float(1.0 / weights[0]),
    }


def split3(value):
    high = value.astype(BF16)
    rest = value - high.astype(F32)
    middle = rest.astype(BF16)
    low = (rest - middle.astype(F32)).astype(BF16)
    return high, middle, low


def mm(a, b):
    return jnp.dot(a, b, preferred_element_type=F32)


def low_half(rows):
    return lax.broadcasted_iota(jnp.int32, (rows, 128), 1) < 64


def swap_halves(value):
    return pltpu.roll(value, 64, 1)


def column_of(row):
    count = row.shape[1]
    spread = jnp.broadcast_to(row.astype(F32), (count, count))
    down = lax.broadcasted_iota(jnp.int32, (count, count), 0)
    across = lax.broadcasted_iota(jnp.int32, (count, count), 1)
    return jnp.sum(jnp.where(down == across, spread, 0.0), axis=1, keepdims=True).astype(jnp.int32)


def slot_row(count):
    at = lax.broadcasted_iota(jnp.int32, (1, count), 1)
    return 6 * (at % 128) + at // 128


def pre_kernel(
    state, send, owner, child, select, restrict, s0, s1, s2, s3, mort, table, large, small
):
    low = low_half(128)
    for pair in range(3):
        fields = [split3(state[2 * pair + side]) for side in range(2)]
        lanes = slice(128 * pair, 128 * pair + 128)
        for piece in range(3):
            even, odd = fields[0][piece], fields[1][piece]
            even_on, odd_on = mm(even, select[...]), mm(odd, select[...])
            first = [even[:, :128].astype(F32), even_on[:, :128], even_on[:, 128:]]
            first_odd = [odd[:, :128].astype(F32), odd_on[:, :128], odd_on[:, 128:]]
            last = [even[:, 384:].astype(F32), even_on[:, :128], even_on[:, 128:]]
            last_odd = [odd[:, 384:].astype(F32), odd_on[:, :128], odd_on[:, 128:]]
            for dim in range(3):
                front = jnp.where(low, first[dim], swap_halves(first_odd[dim]))
                back = jnp.where(low, swap_halves(last[dim]), last_odd[dim])
                table[piece, 256 * dim : 256 * dim + 128, lanes] = front.astype(BF16)
                table[piece, 256 * dim + 128 : 256 * dim + 256, lanes] = back.astype(BF16)
    slots = slot_row(768)
    index = [column_of(send[o : o + 1, :]) for o in range(4)]
    index.append(column_of(owner[...]))
    index += [column_of(child[q : q + 1, :]) for q in range(4)]
    pick = jnp.where(jnp.concatenate(index, 0) == slots, 1.0, 0.0).astype(BF16)
    rows = mm(pick, table[0]) + mm(pick, table[1]) + mm(pick, table[2])
    for o, out in enumerate((s0, s1, s2, s3)):
        out[...] = rows[32 * o : 32 * o + 32]
    large[...] = rows[128:160]
    small[...] = rows[160:288]
    stacked = jnp.concatenate(
        [
            jnp.concatenate(
                [
                    rows[160 + 32 * q : 192 + 32 * q, 128 * part : 128 * part + 128]
                    for q in range(4)
                ],
                1,
            )
            for part in range(3)
        ],
        0,
    )
    back = jnp.dot(stacked, restrict[...], precision=HIGHEST, preferred_element_type=F32)
    for part in range(3):
        mort[pl.ds(part, 32, stride=8), :] = back[32 * part : 32 * part + 32]
        mort[pl.ds(3 + part, 32, stride=8), :] = rows[128:160, 128 * part : 128 * part + 128]
    for part in (6, 7):
        mort[pl.ds(part, 32, stride=8), :] = jnp.zeros((32, 128), F32)


def mid_kernel(
    state, table, source, levels, owner, child, large, both, d0, d1, d2, flux,
    local, remote, own_back, minus_volume,
):
    level = column_of(levels[...])
    twos = (1 << level).astype(F32)
    slots = slot_row(768)
    element = lax.broadcasted_iota(jnp.int32, (128, 1), 0)
    diagonal = lax.broadcasted_iota(
        jnp.int32, (128, 128), 0
    ) == lax.broadcasted_iota(jnp.int32, (128, 128), 1)
    arrived_slot = 768 + lax.broadcasted_iota(jnp.int32, (1, 128), 1)
    child_row = jnp.concatenate([child[q : q + 1, :] for q in range(4)], 1)
    owner_row = owner[...]
    for face in range(6):
        wanted = source[:, face : face + 1]
        mine = 6 * element + face
        rows = slice(128 * face, 128 * face + 128)
        minus = -twos
        blocks = []
        for other in range(6):
            block = jnp.where(wanted == slots[:, 128 * other : 128 * other + 128], minus, 0.0)
            if other == face:
                block = block + jnp.where(diagonal & (wanted >= 0), twos, 0.0)
            blocks.append(block.astype(BF16))
        matrix = jnp.concatenate(blocks, 1)
        local[rows, :] = mm(matrix, table[0]) + mm(matrix, table[1]) + mm(matrix, table[2])
        remote[rows, 0:128] = jnp.where(wanted == arrived_slot, minus, 0.0).astype(BF16)
        remote[rows, 128:256] = jnp.where(mine == child_row, minus, 0.0).astype(BF16)
        remote[rows, 256:288] = jnp.where(mine == owner_row, minus, 0.0).astype(BF16)
    for part in range(3):
        own_back[:, 128 * part : 128 * part + 128] = jnp.dot(
            large[:, 128 * part : 128 * part + 128],
            both[...],
            precision=HIGHEST,
            preferred_element_type=F32,
        )

    def apply(parts, matrix):
        high, middle, low = parts
        small = mm(high, matrix[2]) + mm(middle, matrix[1]) + mm(low, matrix[0])
        return mm(high, matrix[0]) + (mm(high, matrix[1]) + mm(middle, matrix[0]) + small)

    amount = -STEP_SIZE * twos
    grads = []
    for field in range(6):
        parts = split3(state[field])
        along = [apply(parts, d0)]
        for matrix in (d1, d2):
            along.append(
                jnp.concatenate(
                    [apply([p[:, 256 * h : 256 * h + 256] for p in parts], matrix) for h in range(2)],
                    1,
                )
            )
        grads.append(along)
    for out in range(6):
        total = 0.0
        for dim in range(3):
            for field in range(6):
                total = total + flux[dim, out, field] * grads[field][dim]
        minus_volume[out] = amount * total


def post_kernel(
    local, remote, minus_volume, a0, a1, a2, a3, got, small, own_back, project, lift, flux,
    penalty, edge, out,
):
    got_back = [got[pl.ds(part, 32, stride=8), :] for part in range(3)]
    got_large = [got[pl.ds(3 + part, 32, stride=8), :] for part in range(3)]
    onto = jnp.dot(
        jnp.concatenate(got_large, 0), project[...], precision=HIGHEST, preferred_element_type=F32
    )
    child = jnp.concatenate(
        [
            jnp.concatenate(
                [
                    onto[32 * part : 32 * part + 32, 128 * q : 128 * q + 128]
                    for part in range(3)
                ],
                1,
            )
            for q in range(4)
        ],
        0,
    )
    extra = jnp.concatenate(
        [
            a0[...],
            a1[...],
            a2[...],
            a3[...],
            child - small[...],
            jnp.concatenate(got_back, 1) - own_back[...],
        ],
        0,
    )
    parts = split3(extra)
    factor = 0.5 * STEP_SIZE * edge
    low = low_half(128)
    signs = jnp.where(low, -1.0, 1.0)
    surface = [[None] * 3 for _ in range(6)]
    for dim in range(3):
        ends = []
        for side in range(2):
            rows = slice(256 * dim + 128 * side, 256 * dim + 128 * side + 128)
            matrix = remote[rows, :]
            far = mm(matrix, parts[0]) + mm(matrix, parts[1]) + mm(matrix, parts[2])
            ends.append(local[rows, :] + far)
        jumps = []
        for pair in range(3):
            lanes = slice(128 * pair, 128 * pair + 128)
            front, back = ends[0][:, lanes], ends[1][:, lanes]
            jumps.append(jnp.where(low, front, swap_halves(back)))
            jumps.append(jnp.where(low, swap_halves(front), back))
        for field in range(6):
            mixed = (factor * flux[dim, field, 0]) * jumps[0]
            for other in range(1, 6):
                mixed = mixed + (factor * flux[dim, field, other]) * jumps[other]
            surface[field][dim] = signs * mixed - (factor * penalty[field]) * jumps[field]
    for field in range(6):
        lifted = 0.0
        for piece in split3(jnp.concatenate(surface[field][1:], 1)):
            lifted = lifted + mm(piece, lift[...])
        ends = surface[field][0]
        total = minus_volume[field] + lifted
        out[field, :, 0:128] = total[:, 0:128] + jnp.where(low, ends, 0.0)
        out[field, :, 128:384] = total[:, 128:384]
        out[field, :, 384:512] = total[:, 384:512] + jnp.where(low, 0.0, ends)


def per_device(state, levels, face_source, face_send, mort_owner, mort_child, flux_jac, penalty):
    tables = basis_tables(P_SIZE)
    fields_first = state.transpose(1, 0, 2)
    send = face_send.reshape(4, 32)
    owner = mort_owner.reshape(1, 32)
    child = mort_child.transpose(0, 2, 1).reshape(4, 32)

    def shape(dims, kind=F32):
        return jax.ShapeDtypeStruct(dims, kind)

    params = pltpu.CompilerParams(vmem_limit_bytes=28 * MIB)
    s0, s1, s2, s3, mort, table, large, small = pl.pallas_call(
        pre_kernel,
        out_shape=[shape((32, 384))] * 4
        + [
            shape((256, 128)),
            shape((3, 768, 384), BF16),
            shape((32, 384)),
            shape((128, 384)),
        ],
        in_specs=[VMEM] * 6,
        out_specs=[VMEM] * 8,
        compiler_params=params,
        cost_estimate=pl.CostEstimate(flops=10**9, bytes_accessed=4 << 20, transcendentals=0),
        name="pre",
    )(fields_first, send, owner, child, tables["select"], tables["restrict"])
    arrived = [
        shifted(rows, ("gx", "gy"), OFFSETS[place]) for place, rows in enumerate((s0, s1, s2, s3))
    ]
    got = lax.all_to_all(mort.reshape(32, 8, 128), "gy", split_axis=0, concat_axis=0, tiled=True)
    local, remote, own_back, minus_volume = pl.pallas_call(
        mid_kernel,
        out_shape=[
            shape((768, 384)),
            shape((768, 288), BF16),
            shape((32, 384)),
            shape((6, 128, 512)),
        ],
        in_specs=[VMEM] * 11 + [SMEM],
        out_specs=[VMEM] * 4,
        compiler_params=params,
        cost_estimate=pl.CostEstimate(flops=8 * 10**9, bytes_accessed=8 << 20, transcendentals=0),
        name="mid",
    )(
        fields_first,
        table,
        face_source.reshape(128, 6),
        levels.reshape(1, 128),
        owner,
        child,
        large,
        tables["both"],
        tables["deriv_0"],
        tables["deriv_1"],
        tables["deriv_2"],
        flux_jac,
    )
    edge = tables["edge"]

    def post(*refs):
        post_kernel(*refs[:14], edge, refs[14])

    result = pl.pallas_call(
        post,
        out_shape=shape((6, 128, 512)),
        in_specs=[VMEM] * 12 + [SMEM] * 2,
        out_specs=VMEM,
        compiler_params=params,
        cost_estimate=pl.CostEstimate(flops=2 * 10**9, bytes_accessed=4 << 20, transcendentals=0),
        name="post",
    )(
        local,
        remote,
        minus_volume,
        *arrived,
        got.reshape(256, 128),
        small,
        own_back,
        tables["project"],
        tables["lift"],
        flux_jac,
        penalty,
    )
    return result.transpose(1, 0, 2)


def solution(mesh):
    in_specs = (
        P(("gx", "gy"), None, None),
        P(("gx", "gy")),
        P(("gx", "gy")),
        P(("gx", "gy"), None, None),
        P(("gx", "gy"), None, None),
        P(("gx", "gy"), None, None),
        P(),
        P(),
    )
    out_specs = P(("gx", "gy"), None, None)
    return jax.shard_map(
        per_device, mesh=mesh, in_specs=in_specs, out_specs=out_specs, check_vma=False
    )
```

time: 122 us -> 70.7 us (0.58)
  matrix products: 28.8 us -> 0 us
  Pallas kernels: 0 us -> 17.9 us
  local copies, waits for them, and re-layouts: 36.4 us -> 19.6 us
  other arithmetic: 10.2 us -> 0 us
  starting transfers between devices: 38.7 us -> 32.2 us
  waiting for transfers between devices: 6.35 us -> 0.01 us
    dot_general x9 -> x0, matrix products: 28.8 us -> none  [the longest x3 9.48 us: element_rhs(): jnp.dot(flat, deriv_mats[direction], precision=highest)]
    pallas_call x0 -> x3, Pallas kernels: none -> 17.9 us  [the longest x1 10.4 us: per_device(): pl.pallas_call(mid_kernel, out_shape=[shape((768, 384)), shape((768, 288)...]
    unnamed x41 -> x62, local copies, waits for them, and re-layouts: 5.53 us -> 19.5 us
    gather x9 -> x0, local copies, waits for them, and re-layouts: 10.7 us -> none  [the longest x4 4.84 us: per_device(): outgoing = traces[send_rows[place]]]
    reshape x6 -> x1, local copies, waits for them, and re-layouts: 9.34 us -> 0.13 us  [per_device(): face_source.reshape(128, 6)]
    another operation x2 -> x0, local copies, waits for them, and re-layouts: 6.42 us -> none  [the longest x1 6.3 us: element_rhs(): jnp.stack([jnp.dot(flat, deriv_mats[direction], precision=highest) for di...]
    all_to_all x2 -> x1, waiting for transfers between devices: 6.34 us -> 0.01 us  [per_device(): lax.all_to_all(mort.reshape(32, 8, 128), 'gy', split_axis=0, concat_axis=...]
    all_to_all x2 -> x1, starting transfers between devices: 15.6 us -> 10.2 us  [per_device(): lax.all_to_all(mort.reshape(32, 8, 128), 'gy', split_axis=0, concat_axis=...]
  transfers between devices with their start and end apart: 6 -> 5, of which waited for: 1 -> 0; matrix products, arithmetic and copies ran while one was open for 39% -> 0% of each run, Pallas kernels for 0% -> 15%
where the time goes in v1:
time: 70.7 us; the launch traced here: 70 us
  starting transfers between devices  32.2 us (46%)
  local copies, waits for them, and re-layouts  19.6 us (28%)
  Pallas kernels  17.9 us (25%)
    ppermute x4, starting transfers between devices, shifted(): return lax.ppermute(value, axis, pairs)  22.1 us
    unnamed x62, local copies, waits for them, and re-layouts  19.5 us
    pallas_call x1, Pallas kernels, per_device(): pl.pallas_call(mid_kernel, out_shape=[shape((768, 384)), shape((768, 288)...  10.4 us
    all_to_all x1, starting transfers between devices, per_device(): lax.all_to_all(mort.reshape(32, 8, 128), 'gy', split_axis=0, concat_axis=...  10.2 us
    pallas_call x1, Pallas kernels, per_device(): pl.pallas_call(post, out_shape=shape((6, 128, 512)), in_specs=[VMEM] * 12...  4.76 us
    pallas_call x1, Pallas kernels, per_device(): pl.pallas_call(pre_kernel, out_shape=[shape((32, 384))] * 4 + [shape((256...  2.74 us
  transfers between devices with their start and end apart: 5, of which 0 were waited for; matrix products, arithmetic and copies ran while one was open for 0% of the time, Pallas kernels for 15%

profile of v1, /device:TPU:8, one launch (start us, length us, event | category | flops | bytes accessed | tf_op | source)
XLA Modules:
  0.0 70.0 jit_solution(11880049541946538686)
XLA Ops:
  0.0 1.4 %copy-done = f32[128,6,512]{2,0,1:T(8,128)S(1)} copy-done((f32[128,6,512]{2,0,1:T(8,128)S(1)}, f32[128,6,512]{2,0,1:T(8,128)}, u32[]{:S(2)}) %copy-start) | copy-done | bytes 1572888
  2.1 0.7 copy-done.4
  3.4 0.9 %copy-done.15 = f32[512,128]{1,0:T(8,128)S(1)} copy-done((f32[512,128]{1,0:T(8,128)S(1)}, f32[512,128]{1,0:T(8,128)}, u32[]{:S(2)}) %copy-start.15) | copy-done | bytes 262168
  4.4 0.9 %copy-done.16 = bf16[512,256]{1,0:T(8,128)(2,1)S(1)} copy-done((bf16[512,256]{1,0:T(8,128)(2,1)S(1)}, bf16[512,256]{1,0:T(8,128)(2,1)}, u32[]{:S(2)}) %copy-start.16) | copy-done | bytes 262168
  5.4 2.7 %pre.1 = (f32[32,384]{1,0:T(8,128)S(1)}, f32[32,384]{1,0:T(8,128)S(1)}, f32[32,384]{1,0:T(8,128)S(1)}, f32[32,384]{1,0:T(8,128)S(1)}, f32[256,128]{1,0:T(8,128)}...) custom-call(f32[6,128,512]{2,1,0:T(8,128)S(1)} %bitcast.11, ...), custom_call_target="tpu_custom_call" | custom-call | flops 1000000000 | bytes 4194304 | tf_op jit(solution)/shard_map/pre/pallas_call | solution.py:321
  8.1 1.2 %copy-done.20 = bf16[3,768,384]{2,1,0:T(8,128)(2,1)} copy-done((bf16[3,768,384]{2,1,0:T(8,128)(2,1)}, bf16[3,768,384]{2,1,0:T(8,128)(2,1)S(1)}, u32[]{:S(2)}) %copy-start.20) | copy-done | bytes 1769496
  10.0 10.2 %all-to-all-start = ((f32[32,8,128]{2,1,0:T(8,128)}), f32[32,8,128]{2,1,0:T(8,128)S(1)}, u32[]{:S(2)}, u32[]{:S(2)}) async-start(f32[32,8,128]{2,1,0:T(8,128)} %bitcast.6), calls=%async_computation | async-start | bytes 262144 | tf_op jit(solution)/shard_map/all_to_all | solution.py:339
  20.2 14.1 %collective-permute-start = (f32[32,384]{1,0:T(8,128)S(1)}, f32[32,384]{1,0:T(8,128)S(1)}, u32[]{:S(2)}, u32[]{:S(2)}) collective-permute-start(f32[32,384]{1,0:T(8,128)S(1)} %get-tuple-element.22), channel_id=1, source_target_pairs={{0,510},{1,511},{2,0},{3,1},{4,2},{5,3},{6,4},{7,5},{8,6},{9,7},{1... | collective-permute-start | bytes 147464 | tf_op jit(solution)/shard_map/ppermute | solution.py:25
  34.4 3.4 %collective-permute-start.1 = (f32[32,384]{1,0:T(8,128)S(1)}, f32[32,384]{1,0:T(8,128)S(1)}, u32[]{:S(2)}, u32[]{:S(2)}) collective-permute-start(f32[32,384]{1,0:T(8,128)S(1)} %get-tuple-element.23), channel_id=1, source_target_pairs={{0,511},{1,0},{2,1},{3,2},{4,3},{5,4},{6,5},{7,6},{8,7},{9,8},{10,... | collective-permute-start | bytes 147464 | tf_op jit(solution)/shard_map/ppermute | solution.py:25
  37.7 2.5 %collective-permute-start.2 = (f32[32,384]{1,0:T(8,128)S(1)}, f32[32,384]{1,0:T(8,128)S(1)}, u32[]{:S(2)}, u32[]{:S(2)}) collective-permute-start(f32[32,384]{1,0:T(8,128)S(1)} %get-tuple-element.24), channel_id=1, source_target_pairs={{0,1},{1,2},{2,3},{3,4},{4,5},{5,6},{6,7},{7,8},{8,9},{9,10},{10,1... | collective-permute-start | bytes 147464 | tf_op jit(solution)/shard_map/ppermute | solution.py:25
  40.2 2.1 %collective-permute-start.3 = (f32[32,384]{1,0:T(8,128)S(1)}, f32[32,384]{1,0:T(8,128)S(1)}, u32[]{:S(2)}, u32[]{:S(2)}) collective-permute-start(f32[32,384]{1,0:T(8,128)S(1)} %get-tuple-element.25), channel_id=1, source_target_pairs={{0,2},{1,3},{2,4},{3,5},{4,6},{5,7},{6,8},{7,9},{8,10},{9,11},{10,... | collective-permute-start | bytes 147464 | tf_op jit(solution)/shard_map/ppermute | solution.py:25
  42.6 1.4 %copy-done.10 = bf16[3,512,512]{2,1,0:T(8,128)(2,1)S(1)} copy-done((bf16[3,512,512]{2,1,0:T(8,128)(2,1)S(1)}, bf16[3,512,512]{2,1,0:T(8,128)(2,1)}, u32[]{:S(2)}) %copy-start.10) | copy-done | bytes 1572888
  44.0 0.8 %copy-done.17 = f32[128,128]{1,0:T(8,128)S(1)} copy-done((f32[128,128]{1,0:T(8,128)S(1)}, f32[128,128]{1,0:T(8,128)}, u32[]{:S(2)}) %copy-start.17) | copy-done | bytes 65560
  44.8 1.5 %copy-done.21 = bf16[3,768,384]{2,1,0:T(8,128)(2,1)S(1)} copy-done((bf16[3,768,384]{2,1,0:T(8,128)(2,1)S(1)}, bf16[3,768,384]{2,1,0:T(8,128)(2,1)}, u32[]{:S(2)}) %copy-start.21) | copy-done | bytes 1769496
  46.3 0.8 %copy-done.29 = f32[32,384]{1,0:T(8,128)S(1)} copy-done((f32[32,384]{1,0:T(8,128)S(1)}, f32[32,384]{1,0:T(8,128)}, u32[]{:S(2)}) %copy-start.29) | copy-done | bytes 49176
  47.1 10.4 %mid.1 = (f32[768,384]{1,0:T(8,128)S(1)}, bf16[768,288]{1,0:T(8,128)(2,1)S(1)}, f32[32,384]{1,0:T(8,128)S(1)}, f32[6,128,512]{2,1,0:T(8,128)S(1)}) custom-call(f32[6,128,512]{2,1,0:T(8,128)S(1)} %bitcast.12, bf16[3,768,384]{2,1,0:T(8,128)(2,1)S(1)} %copy-done.21, s32[128,6]{1,0:T(8,128)S(1)} %reshape.24.source, s32[1,128]{1,0:T(1,128)S(1)} %bitcast.18, ...), custom_call_target="tpu_custom_call" | custom-call | flops 8000000000 | bytes 8388608 | tf_op jit(solution)/shard_map/mid/pallas_call | solution.py:340
  57.5 1.1 %copy-done.18 = f32[6,128,512]{2,1,0:T(8,128)} copy-done((f32[6,128,512]{2,1,0:T(8,128)}, f32[6,128,512]{2,1,0:T(8,128)S(1)}, u32[]{:S(2)}) %copy-start.18) | copy-done | bytes 1572888
  58.6 1.0 %copy-done.22 = f32[768,384]{1,0:T(8,128)} copy-done((f32[768,384]{1,0:T(8,128)}, f32[768,384]{1,0:T(8,128)S(1)}, u32[]{:S(2)}) %copy-start.22) | copy-done | bytes 1179672
  59.7 0.8 %copy-done.24 = bf16[768,288]{1,0:T(8,128)(2,1)} copy-done((bf16[768,288]{1,0:T(8,128)(2,1)}, bf16[768,288]{1,0:T(8,128)(2,1)S(1)}, u32[]{:S(2)}) %copy-start.24) | copy-done | bytes 442392
  60.6 1.4 %copy-done.19 = f32[6,128,512]{2,1,0:T(8,128)S(1)} copy-done((f32[6,128,512]{2,1,0:T(8,128)S(1)}, f32[6,128,512]{2,1,0:T(8,128)}, u32[]{:S(2)}) %copy-start.19) | copy-done | bytes 1572888
  62.0 1.3 %copy-done.23 = f32[768,384]{1,0:T(8,128)S(1)} copy-done((f32[768,384]{1,0:T(8,128)S(1)}, f32[768,384]{1,0:T(8,128)}, u32[]{:S(2)}) %copy-start.23) | copy-done | bytes 1179672
  63.2 1.1 %copy-done.25 = bf16[768,288]{1,0:T(8,128)(2,1)S(1)} copy-done((bf16[768,288]{1,0:T(8,128)(2,1)S(1)}, bf16[768,288]{1,0:T(8,128)(2,1)}, u32[]{:S(2)}) %copy-start.25) | copy-done | bytes 442392
  64.3 0.9 %copy-done.27 = f32[128,384]{1,0:T(8,128)S(1)} copy-done((f32[128,384]{1,0:T(8,128)S(1)}, f32[128,384]{1,0:T(8,128)}, u32[]{:S(2)}) %copy-start.27) | copy-done | bytes 196632
  65.2 4.8 %post.1 = f32[6,128,512]{2,1,0:T(8,128)} custom-call(f32[768,384]{1,0:T(8,128)S(1)} %copy-done.23, bf16[768,288]{1,0:T(8,128)(2,1)S(1)} %copy-done.25, f32[6,128,512]{2,1,0:T(8,128)S(1)} %copy-done.19, f32[32,384]{1,0:T(8,128)S(1)} %collective-permute-done.refs_3_, f32[32,384]{1,0:T(8,128)S(1)} %collective-permute-done.1.refs_4_, ...), custom_call_target="tpu_custom_call" | custom-call | flops 2000000000 | bytes 4194304 | tf_op jit(solution)/shard_map/post/pallas_call | solution.py:372
  (52 shorter events, 2.2 us)
Async XLA Ops:
  0.0 1.4 %copy-start = (f32[128,6,512]{2,0,1:T(8,128)S(1)}, f32[128,6,512]{2,0,1:T(8,128)}, u32[]{:S(2)}) copy-start(f32[128,6,512]{2,0,1:T(8,128)} %param.16) | copy-start | bytes 4718596
  5.3 37.0 %copy-start.30 = (s32[768]{0:T(1024)S(1)}, s32[768]{0:T(1024)}, u32[]{:S(2)}) copy-start(s32[768]{0:T(1024)} %param.18) | copy-start | bytes 9220
  5.3 37.2 %copy-start.1 = (f32[128,6,512]{2,0,1:T(8,128)S(1)}, f32[128,6,512]{2,0,1:T(8,128)}, u32[]{:S(2)}) copy-start(f32[128,6,512]{2,0,1:T(8,128)} %param.16) | copy-start | bytes 4718596
  5.3 37.2 %copy-start.2 = (f32[3,6,6]{2,1,0:T(8,128)S(1)}, f32[3,6,6]{2,1,0:T(8,128)}, u32[]{:S(2)}) copy-start(f32[3,6,6]{2,1,0:T(8,128)} %refs_12_.1) | copy-start | bytes 1300
  5.3 37.2 %copy-start.5 = (s32[1,32,4]{1,2,0:T(4,128)S(1)}, s32[1,32,4]{1,2,0:T(4,128)}, u32[]{:S(2)}) copy-start(s32[1,32,4]{1,2,0:T(4,128)} %param.21) | copy-start | bytes 1540
  5.3 37.2 %copy-start.7 = (s32[1,32,1]{1,2,0:T(1,128)S(1)}, s32[1,32,1]{1,2,0:T(1,128)}, u32[]{:S(2)}) copy-start(s32[1,32,1]{1,2,0:T(1,128)} %param.20) | copy-start | bytes 388
  5.4 37.2 %copy-start.8 = (s32[128]{0:T(128)S(1)}, s32[128]{0:T(128)}, u32[]{:S(2)}) copy-start(s32[128]{0:T(128)} %param.17) | copy-start | bytes 1540
  5.4 37.2 %copy-start.11 = (bf16[3,256,256]{2,1,0:T(8,128)(2,1)S(1)}, bf16[3,256,256]{2,1,0:T(8,128)(2,1)}, u32[]{:S(2)}) copy-start(bf16[3,256,256]{2,1,0:T(8,128)(2,1)} %constant.21.clone.d2) | copy-start | bytes 1179652
  5.4 37.2 %copy-start.12 = (bf16[3,256,256]{2,1,0:T(8,128)(2,1)S(1)}, bf16[3,256,256]{2,1,0:T(8,128)(2,1)}, u32[]{:S(2)}) copy-start(bf16[3,256,256]{2,1,0:T(8,128)(2,1)} %constant.20.clone.d1) | copy-start | bytes 1179652
  8.1 1.2 %copy-start.20 = (bf16[3,768,384]{2,1,0:T(8,128)(2,1)}, bf16[3,768,384]{2,1,0:T(8,128)(2,1)S(1)}, u32[]{:S(2)}) copy-start(bf16[3,768,384]{2,1,0:T(8,128)(2,1)S(1)} %get-tuple-element.17.table) | copy-start | bytes 5308420
  10.0 10.2 %copy-start.28 = (f32[32,384]{1,0:T(8,128)}, f32[32,384]{1,0:T(8,128)S(1)}, u32[]{:S(2)}) copy-start(f32[32,384]{1,0:T(8,128)S(1)} %get-tuple-element.18.large) | copy-start | bytes 147460
  10.0 50.5 %all-to-all-start = ((f32[32,8,128]{2,1,0:T(8,128)}), f32[32,8,128]{2,1,0:T(8,128)S(1)}, u32[]{:S(2)}, u32[]{:S(2)}) async-start(f32[32,8,128]{2,1,0:T(8,128)} %bitcast.6), calls=%async_computation | async-start | bytes 262144 | tf_op jit(solution)/shard_map/all_to_all | solution.py:339
  20.2 40.3 %collective-permute-start = (f32[32,384]{1,0:T(8,128)S(1)}, f32[32,384]{1,0:T(8,128)S(1)}, u32[]{:S(2)}, u32[]{:S(2)}) collective-permute-start(f32[32,384]{1,0:T(8,128)S(1)} %get-tuple-element.22), channel_id=1, source_target_pairs={{0,510},{1,511},{2,0},{3,1},{4,2},{5,3},{6,4},{7,5},{8,6},{9,7},{1... | collective-permute-start | bytes 147464 | tf_op jit(solution)/shard_map/ppermute | solution.py:25
  34.4 26.1 %collective-permute-start.1 = (f32[32,384]{1,0:T(8,128)S(1)}, f32[32,384]{1,0:T(8,128)S(1)}, u32[]{:S(2)}, u32[]{:S(2)}) collective-permute-start(f32[32,384]{1,0:T(8,128)S(1)} %get-tuple-element.23), channel_id=1, source_target_pairs={{0,511},{1,0},{2,1},{3,2},{4,3},{5,4},{6,5},{7,6},{8,7},{9,8},{10,... | collective-permute-start | bytes 147464 | tf_op jit(solution)/shard_map/ppermute | solution.py:25
  37.7 22.8 %collective-permute-start.2 = (f32[32,384]{1,0:T(8,128)S(1)}, f32[32,384]{1,0:T(8,128)S(1)}, u32[]{:S(2)}, u32[]{:S(2)}) collective-permute-start(f32[32,384]{1,0:T(8,128)S(1)} %get-tuple-element.24), channel_id=1, source_target_pairs={{0,1},{1,2},{2,3},{3,4},{4,5},{5,6},{6,7},{7,8},{8,9},{9,10},{10,1... | collective-permute-start | bytes 147464 | tf_op jit(solution)/shard_map/ppermute | solution.py:25
  40.2 20.3 %collective-permute-start.3 = (f32[32,384]{1,0:T(8,128)S(1)}, f32[32,384]{1,0:T(8,128)S(1)}, u32[]{:S(2)}, u32[]{:S(2)}) collective-permute-start(f32[32,384]{1,0:T(8,128)S(1)} %get-tuple-element.25), channel_id=1, source_target_pairs={{0,2},{1,3},{2,4},{3,5},{4,6},{5,7},{6,8},{7,9},{8,10},{9,11},{10,... | collective-permute-start | bytes 147464 | tf_op jit(solution)/shard_map/ppermute | solution.py:25
  42.6 1.4 %copy-start.10 = (bf16[3,512,512]{2,1,0:T(8,128)(2,1)S(1)}, bf16[3,512,512]{2,1,0:T(8,128)(2,1)}, u32[]{:S(2)}) copy-start(bf16[3,512,512]{2,1,0:T(8,128)(2,1)} %constant.19.clone.d0) | copy-start | bytes 4718596
  44.8 1.5 %copy-start.21 = (bf16[3,768,384]{2,1,0:T(8,128)(2,1)S(1)}, bf16[3,768,384]{2,1,0:T(8,128)(2,1)}, u32[]{:S(2)}) copy-start(bf16[3,768,384]{2,1,0:T(8,128)(2,1)} %copy-done.20) | copy-start | bytes 5308420
  47.1 13.4 %copy-start.9 = (f32[6]{0:T(128)S(1)}, f32[6]{0:T(128)}, u32[]{:S(2)}) copy-start(f32[6]{0:T(128)} %refs_13_.1) | copy-start | bytes 76
  47.1 13.4 %copy-start.13 = (bf16[256,512]{1,0:T(8,128)(2,1)S(1)}, bf16[256,512]{1,0:T(8,128)(2,1)}, u32[]{:S(2)}) copy-start(bf16[256,512]{1,0:T(8,128)(2,1)} %constant.23.clone.refs_11_) | copy-start | bytes 786436
  47.1 13.5 %copy-start.14 = (f32[128,512]{1,0:T(8,128)S(1)}, f32[128,512]{1,0:T(8,128)}, u32[]{:S(2)}) copy-start(f32[128,512]{1,0:T(8,128)} %constant.22.clone.refs_10_) | copy-start | bytes 786436
  57.5 1.1 %copy-start.18 = (f32[6,128,512]{2,1,0:T(8,128)}, f32[6,128,512]{2,1,0:T(8,128)S(1)}, u32[]{:S(2)}) copy-start(f32[6,128,512]{2,1,0:T(8,128)S(1)} %get-tuple-element.21.refs_2_) | copy-start | bytes 4718596
  60.6 1.4 %copy-start.19 = (f32[6,128,512]{2,1,0:T(8,128)S(1)}, f32[6,128,512]{2,1,0:T(8,128)}, u32[]{:S(2)}) copy-start(f32[6,128,512]{2,1,0:T(8,128)} %copy-done.18) | copy-start | bytes 4718596
  62.0 1.3 %copy-start.23 = (f32[768,384]{1,0:T(8,128)S(1)}, f32[768,384]{1,0:T(8,128)}, u32[]{:S(2)}) copy-start(f32[768,384]{1,0:T(8,128)} %copy-done.22) | copy-start | bytes 3538948
  (12 other events, 10.1 us)

commit v2 on v1

v2 whole, which is shorter than its diff:
```python
import jax
import jax.numpy as jnp
import ml_dtypes
import numpy as np
from jax import lax
from jax.experimental import pallas as pl
from jax.experimental.pallas import tpu as pltpu
from jax.sharding import PartitionSpec as P

P_SIZE = 7
OFFSETS = (-2, -1, 1, 2)
STEP_SIZE = 0.01

F32 = jnp.float32
BF16 = jnp.bfloat16
HIGHEST = lax.Precision.HIGHEST
VMEM = pl.BlockSpec(memory_space=pltpu.VMEM)
HBM = pl.BlockSpec(memory_space=pltpu.HBM)
SMEM = pl.BlockSpec(memory_space=pltpu.SMEM)
MIB = 1 << 20


def shifted(value, axis, steps):
    count = lax.axis_size(axis)
    pairs = [(source, (source + steps) % count) for source in range(count)]
    return lax.ppermute(value, axis, pairs)


def pieces_of(table):
    rest = np.asarray(table, np.float32)
    out = []
    for _ in range(2):
        piece = rest.astype(ml_dtypes.bfloat16)
        out.append(piece)
        rest = rest - piece.astype(np.float32)
    return np.stack(out)


def basis_tables(order):
    per_dim = order + 1
    eye_small = np.eye(per_dim)
    points = -np.cos(np.pi * np.arange(per_dim) / order)
    differences = points[:, None] - points[None, :] + eye_small
    barycentric = 1.0 / np.prod(differences, axis=1)
    derivative = barycentric[None, :] / barycentric[:, None] / differences
    derivative = np.where(eye_small > 0, 0.0, derivative)
    derivative = derivative - eye_small * derivative.sum(axis=1)[:, None]
    angles = np.pi * np.arange(per_dim) / order
    weights = np.ones(per_dim)
    for wave in range(1, order // 2 + 1):
        factor = 1.0 if 2 * wave == order else 2.0
        weights = weights - factor * np.cos(2.0 * wave * angles) / (4.0 * wave * wave - 1.0)
    edge_factor = np.where((np.arange(per_dim) == 0) | (np.arange(per_dim) == order), 1.0, 2.0)
    weights = edge_factor * weights / order

    def lagrange(targets):
        values_at = np.ones((per_dim, per_dim))
        for column in range(per_dim):
            for other in range(per_dim):
                if other != column:
                    values_at[:, column] *= (targets - points[other]) / (
                        points[column] - points[other]
                    )
        return values_at

    halves = [lagrange((points - 1.0) / 2.0), lagrange((points + 1.0) / 2.0)]
    identity = np.eye(per_dim)
    node_index = np.arange(per_dim**3).reshape(per_dim, per_dim, per_dim)
    fnodes = per_dim * per_dim
    select = np.zeros((per_dim**3, 4 * fnodes), np.float32)
    for face in range(2, 6):
        picker = [slice(None), slice(None), slice(None)]
        picker[face // 2] = 0 if face % 2 == 0 else order
        on_face = node_index[tuple(picker)].reshape(-1)
        select[on_face, (face - 2) * fnodes + np.arange(fnodes)] = 1.0
    face_weight = np.kron(weights, weights)
    proj = [np.kron(halves[quad // 2], halves[quad % 2]) for quad in range(4)]
    restrict = [
        0.25 * (proj[quad].T * face_weight[None, :]) / face_weight[:, None] for quad in range(4)
    ]
    two = np.eye(2)
    both = sum(restrict[quad] @ proj[quad] for quad in range(4))
    quarter = np.eye(4)
    return {
        "select": select.astype(ml_dtypes.bfloat16),
        "lift": np.ascontiguousarray(select.T).astype(ml_dtypes.bfloat16),
        "restrict": np.concatenate([np.kron(two, r.T) for r in restrict], 0).astype(np.float32),
        "project": np.concatenate([np.kron(two, p.T) for p in proj], 1).astype(np.float32),
        "both": np.kron(two, both.T).astype(np.float32),
        "deriv_0": pieces_of(np.kron(derivative, np.eye(fnodes)).T),
        "deriv_1": pieces_of(np.kron(quarter, np.kron(derivative, identity)).T),
        "deriv_2": pieces_of(np.kron(quarter, np.kron(identity, derivative)).T),
        "edge": float(1.0 / weights[0]),
    }


def split3(value):
    high = value.astype(BF16)
    rest = value - high.astype(F32)
    middle = rest.astype(BF16)
    low = (rest - middle.astype(F32)).astype(BF16)
    return high, middle, low


def mm(a, b):
    return jnp.dot(a, b, preferred_element_type=F32)


def low_half(rows):
    return lax.broadcasted_iota(jnp.int32, (rows, 128), 1) < 64


def swap_halves(value):
    return pltpu.roll(value, 64, 1)


def column_of(row):
    count = row.shape[1]
    spread = jnp.broadcast_to(row.astype(F32), (count, count))
    down = lax.broadcasted_iota(jnp.int32, (count, count), 0)
    across = lax.broadcasted_iota(jnp.int32, (count, count), 1)
    return jnp.sum(jnp.where(down == across, spread, 0.0), axis=1, keepdims=True).astype(jnp.int32)


def slot_row(count):
    at = lax.broadcasted_iota(jnp.int32, (1, count), 1)
    return 6 * (at % 128) + at // 128


def start_all(sources, targets, arrivals):
    copies = [
        pltpu.make_async_copy(source, target, arrivals.at[at])
        for at, (source, target) in enumerate(zip(sources, targets, strict=True))
    ]
    for copy in copies:
        copy.start()
    return copies


def rows_of(field):
    return slice(128 * field, 128 * field + 128)


def pre_kernel(
    state_far, send_far, owner_far, child_far, select_far, restrict_far,
    s0_far, s1_far, s2_far, s3_far, mort_far, table_far, large_far, small_far,
    state, send, owner, child, select, restrict, ends, pieces, table, picked, mort, arrivals, sent,
):
    copies = start_all(
        [select_far, *(state_far.at[rows_of(f)] for f in range(6)), send_far, owner_far, child_far, restrict_far],
        [select, *(state.at[rows_of(f)] for f in range(6)), send, owner, child, restrict],
        arrivals,
    )
    low = low_half(128)
    for field in range(6):
        copies[1 + field].wait()
        rows = rows_of(field)
        for piece, value in enumerate(split3(state[rows])):
            pieces[piece, rows] = value
            ends[piece, rows, :128] = value[:, :128].astype(F32)
            ends[piece, rows, 128:] = value[:, 384:].astype(F32)
    copies[0].wait()
    for piece in range(3):
        inner = mm(pieces[piece], select[...])
        for pair in range(3):
            even, odd = rows_of(2 * pair), rows_of(2 * pair + 1)
            lanes = slice(128 * pair, 128 * pair + 128)
            fronts = [(ends[piece, even, :128], ends[piece, odd, :128])]
            backs = [(ends[piece, even, 128:], ends[piece, odd, 128:])]
            for dim in range(2):
                at = slice(128 * dim, 128 * dim + 128)
                fronts.append((inner[even, at], inner[odd, at]))
            backs += fronts[1:]
            for dim in range(3):
                front = jnp.where(low, fronts[dim][0], swap_halves(fronts[dim][1]))
                back = jnp.where(low, swap_halves(backs[dim][0]), backs[dim][1])
                table[piece, 256 * dim : 256 * dim + 128, lanes] = front.astype(BF16)
                table[piece, 256 * dim + 128 : 256 * dim + 256, lanes] = back.astype(BF16)
    leaving = start_all([table], [table_far], sent)
    for copy in copies[7:]:
        copy.wait()
    slots = slot_row(768)
    index = [column_of(send[o : o + 1, :]) for o in range(4)]
    index.append(column_of(owner[...]))
    index += [column_of(child[q : q + 1, :]) for q in range(4)]
    pick = jnp.where(jnp.concatenate(index, 0) == slots, 1.0, 0.0).astype(BF16)
    picked[...] = mm(pick, table[0]) + mm(pick, table[1]) + mm(pick, table[2])
    leaving += start_all(
        [*(picked.at[32 * o : 32 * o + 32] for o in range(4)), picked.at[128:160], picked.at[160:288]],
        [s0_far, s1_far, s2_far, s3_far, large_far, small_far],
        sent.at[1:7],
    )
    stacked = jnp.concatenate(
        [
            jnp.concatenate(
                [
                    picked[160 + 32 * q : 192 + 32 * q, 128 * part : 128 * part + 128]
                    for q in range(4)
                ],
                1,
            )
            for part in range(3)
        ],
        0,
    )
    back = jnp.dot(stacked, restrict[...], precision=HIGHEST, preferred_element_type=F32)
    for part in range(3):
        mort[pl.ds(part, 32, stride=8), :] = back[32 * part : 32 * part + 32]
        mort[pl.ds(3 + part, 32, stride=8), :] = picked[128:160, 128 * part : 128 * part + 128]
    for part in (6, 7):
        mort[pl.ds(part, 32, stride=8), :] = jnp.zeros((32, 128), F32)
    leaving += start_all([mort], [mort_far], sent.at[7:8])
    for copy in leaving:
        copy.wait()


def mid_kernel(
    levels_far, owner_far, child_far, source_far, state_far, d0_far, d1_far, d2_far, table_far,
    large_far, both_far, flux, local_far, remote_far, own_back_far, minus_volume_far,
    levels, owner, child, source, state, d0, d1, d2, table, large, both, local, remote, own_back,
    minus_volume, pieces, grads, matrix, amount, arrivals, sent,
):
    copies = start_all(
        [levels_far, owner_far, child_far, source_far, state_far, d0_far, d1_far, d2_far, table_far, large_far, both_far],
        [levels, owner, child, source, state, d0, d1, d2, table, large, both],
        arrivals,
    )
    for copy in copies[:4]:
        copy.wait()
    level = column_of(levels[...])
    twos = (1 << level).astype(F32)
    minus = -twos
    amount[...] = jnp.broadcast_to(minus * STEP_SIZE, (128, 128))
    slots = slot_row(768)
    element = lax.broadcasted_iota(jnp.int32, (128, 1), 0)
    diagonal = lax.broadcasted_iota(
        jnp.int32, (128, 128), 0
    ) == lax.broadcasted_iota(jnp.int32, (128, 128), 1)
    arrived_slot = 768 + lax.broadcasted_iota(jnp.int32, (1, 128), 1)
    child_row = jnp.concatenate([child[q : q + 1, :] for q in range(4)], 1)
    owner_row = owner[...]
    for face in range(6):
        wanted = source[:, face : face + 1]
        mine = 6 * element + face
        rows = rows_of(face)
        for other in range(6):
            block = jnp.where(wanted == slots[:, rows_of(other)], minus, 0.0)
            if other == face:
                block = block + jnp.where(diagonal & (wanted >= 0), twos, 0.0)
            matrix[rows, rows_of(other)] = block.astype(BF16)
        remote[rows, 0:128] = jnp.where(wanted == arrived_slot, minus, 0.0).astype(BF16)
        remote[rows, 128:256] = jnp.where(mine == child_row, minus, 0.0).astype(BF16)
        remote[rows, 256:288] = jnp.where(mine == owner_row, minus, 0.0).astype(BF16)
    leaving = start_all([remote], [remote_far], sent)
    copies[4].wait()
    for field in range(6):
        rows = rows_of(field)
        value = state[rows]
        high = value.astype(BF16)
        pieces[0, rows] = high
        pieces[1, rows] = (value - high.astype(F32)).astype(BF16)
    for copy in copies[5:8]:
        copy.wait()

    def apply(lanes, deriv):
        high, rest = pieces[0, :, lanes], pieces[1, :, lanes]
        return mm(high, deriv[0]) + (mm(high, deriv[1]) + mm(rest, deriv[0]))

    grads[0] = apply(slice(0, 512), d0)
    for half in range(2):
        lanes = slice(256 * half, 256 * half + 256)
        grads[1, :, lanes] = apply(lanes, d1)
        grads[2, :, lanes] = apply(lanes, d2)

    def mix(step, carry):
        first = pl.multiple_of(8 * step, 8)
        scale = amount[pl.ds(first, 8), :]
        scale = jnp.concatenate([scale, scale], 1)
        for half in range(2):
            lanes = slice(256 * half, 256 * half + 256)
            parts = [
                [grads[dim, pl.ds(128 * field + first, 8), lanes] for field in range(6)]
                for dim in range(3)
            ]
            for out in range(6):
                total = flux[0, out, 0] * parts[0][0]
                for dim in range(3):
                    for field in range(6):
                        if dim + field:
                            total = total + flux[dim, out, field] * parts[dim][field]
                minus_volume[pl.ds(128 * out + first, 8), lanes] = scale * total
        return carry

    lax.fori_loop(0, 16, mix, 0)
    leaving += start_all([minus_volume], [minus_volume_far], sent.at[1:2])
    for copy in copies[8:]:
        copy.wait()
    local[...] = (
        mm(matrix[...], table[0]) + mm(matrix[...], table[1]) + mm(matrix[...], table[2])
    )
    leaving += start_all([local], [local_far], sent.at[2:3])
    for part in range(3):
        own_back[:, 128 * part : 128 * part + 128] = jnp.dot(
            large[:, 128 * part : 128 * part + 128],
            both[...],
            precision=HIGHEST,
            preferred_element_type=F32,
        )
    leaving += start_all([own_back], [own_back_far], sent.at[3:4])
    for copy in leaving:
        copy.wait()


def post_kernel(
    got_far, project_far, a0_far, a1_far, a2_far, a3_far, small_far, own_back_far, remote_far,
    local_far, lift_far, minus_volume_far, flux, penalty, edge, out_far,
    got, project, arrived, small, own_back, remote, local, lift, minus_volume,
    jumps, ends, pieces, out, arrivals, done,
):
    copies = start_all(
        [got_far, project_far, a0_far, a1_far, a2_far, a3_far, small_far, own_back_far, remote_far, local_far, lift_far, minus_volume_far],
        [got, project, *(arrived.at[32 * o : 32 * o + 32] for o in range(4)), small, own_back, remote, local, lift, minus_volume],
        arrivals,
    )
    for copy in copies[:8]:
        copy.wait()
    got_back = [got[pl.ds(part, 32, stride=8), :] for part in range(3)]
    got_large = [got[pl.ds(3 + part, 32, stride=8), :] for part in range(3)]
    onto = jnp.dot(
        jnp.concatenate(got_large, 0), project[...], precision=HIGHEST, preferred_element_type=F32
    )
    child = jnp.concatenate(
        [
            jnp.concatenate(
                [
                    onto[32 * part : 32 * part + 32, 128 * q : 128 * q + 128]
                    for part in range(3)
                ],
                1,
            )
            for q in range(4)
        ],
        0,
    )
    extra = jnp.concatenate(
        [
            arrived[...],
            child - small[...],
            jnp.concatenate(got_back, 1) - own_back[...],
        ],
        0,
    )
    parts = split3(extra)
    copies[8].wait()
    copies[9].wait()
    picks = remote[...]
    jumps[...] = local[...] + (mm(picks, parts[0]) + mm(picks, parts[1]) + mm(picks, parts[2]))
    factor = 0.5 * STEP_SIZE * edge
    step = 16
    low = low_half(step)
    signs = jnp.where(low, -1.0, 1.0)
    for dim in range(3):
        rates = [[factor * flux[dim, g, h] for h in range(6)] for g in range(6)]
        drags = [factor * penalty[g] for g in range(6)]
        for first in range(0, 128, step):
            values = []
            for pair in range(3):
                lanes = slice(128 * pair, 128 * pair + 128)
                front = jumps[256 * dim + first : 256 * dim + first + step, lanes]
                back = jumps[256 * dim + 128 + first : 256 * dim + 128 + first + step, lanes]
                values.append(jnp.where(low, front, swap_halves(back)))
                values.append(jnp.where(low, swap_halves(front), back))
            for field in range(6):
                mixed = rates[field][0] * values[0]
                for other in range(1, 6):
                    mixed = mixed + rates[field][other] * values[other]
                surface = signs * mixed - drags[field] * values[field]
                rows = slice(128 * field + first, 128 * field + first + step)
                if dim == 0:
                    ends[rows] = surface
                else:
                    for piece, value in enumerate(split3(surface)):
                        pieces[piece, rows, 128 * dim - 128 : 128 * dim] = value
    copies[10].wait()
    copies[11].wait()
    low = low_half(256)
    sent = []
    for pair in range(3):
        rows = slice(256 * pair, 256 * pair + 256)
        lifted = mm(pieces[0, rows], lift[...])
        lifted = lifted + mm(pieces[1, rows], lift[...])
        lifted = lifted + mm(pieces[2, rows], lift[...])
        total = minus_volume[rows] + lifted
        edges = ends[rows]
        out[rows, 0:128] = total[:, 0:128] + jnp.where(low, edges, 0.0)
        out[rows, 128:384] = total[:, 128:384]
        out[rows, 384:512] = total[:, 384:512] + jnp.where(low, 0.0, edges)
        copy = pltpu.make_async_copy(out.at[rows], out_far.at[rows], done.at[pair])
        copy.start()
        sent.append(copy)
    for copy in sent:
        copy.wait()


def per_device(state, levels, face_source, face_send, mort_owner, mort_child, flux_jac, penalty):
    tables = basis_tables(P_SIZE)
    by_field = state.transpose(1, 0, 2).reshape(768, 512)
    send = face_send.reshape(4, 32)
    owner = mort_owner.reshape(1, 32)
    child = mort_child.transpose(0, 2, 1).reshape(4, 32)

    def shape(dims, kind=F32):
        return jax.ShapeDtypeStruct(dims, kind)

    params = pltpu.CompilerParams(vmem_limit_bytes=60 * MIB)
    s0, s1, s2, s3, mort, table, large, small = pl.pallas_call(
        pre_kernel,
        out_shape=[shape((32, 384))] * 4
        + [
            shape((256, 128)),
            shape((3, 768, 384), BF16),
            shape((32, 384)),
            shape((128, 384)),
        ],
        in_specs=[HBM] * 6,
        out_specs=[HBM] * 8,
        scratch_shapes=[
            pltpu.VMEM((768, 512), F32),
            pltpu.VMEM((4, 32), jnp.int32),
            pltpu.VMEM((1, 32), jnp.int32),
            pltpu.VMEM((4, 32), jnp.int32),
            pltpu.VMEM((512, 256), BF16),
            pltpu.VMEM((512, 128), F32),
            pltpu.VMEM((3, 768, 256), F32),
            pltpu.VMEM((3, 768, 512), BF16),
            pltpu.VMEM((3, 768, 384), BF16),
            pltpu.VMEM((288, 384), F32),
            pltpu.VMEM((256, 128), F32),
            pltpu.SemaphoreType.DMA((11,)),
            pltpu.SemaphoreType.DMA((8,)),
        ],
        compiler_params=params,
        cost_estimate=pl.CostEstimate(flops=10**9, bytes_accessed=4 << 20, transcendentals=0),
        name="pre",
    )(by_field, send, owner, child, tables["select"], tables["restrict"])
    arrived = [
        shifted(rows, ("gx", "gy"), OFFSETS[place]) for place, rows in enumerate((s0, s1, s2, s3))
    ]
    got = lax.all_to_all(mort.reshape(32, 8, 128), "gy", split_axis=0, concat_axis=0, tiled=True)
    local, remote, own_back, minus_volume = pl.pallas_call(
        mid_kernel,
        out_shape=[
            shape((768, 384)),
            shape((768, 288), BF16),
            shape((32, 384)),
            shape((768, 512)),
        ],
        in_specs=[HBM] * 11 + [SMEM],
        out_specs=[HBM] * 4,
        scratch_shapes=[
            pltpu.VMEM((1, 128), jnp.int32),
            pltpu.VMEM((1, 32), jnp.int32),
            pltpu.VMEM((4, 32), jnp.int32),
            pltpu.VMEM((128, 6), jnp.int32),
            pltpu.VMEM((768, 512), F32),
            pltpu.VMEM((2, 512, 512), BF16),
            pltpu.VMEM((2, 256, 256), BF16),
            pltpu.VMEM((2, 256, 256), BF16),
            pltpu.VMEM((3, 768, 384), BF16),
            pltpu.VMEM((32, 384), F32),
            pltpu.VMEM((128, 128), F32),
            pltpu.VMEM((768, 384), F32),
            pltpu.VMEM((768, 288), BF16),
            pltpu.VMEM((32, 384), F32),
            pltpu.VMEM((768, 512), F32),
            pltpu.VMEM((2, 768, 512), BF16),
            pltpu.VMEM((3, 768, 512), F32),
            pltpu.VMEM((768, 768), BF16),
            pltpu.VMEM((128, 128), F32),
            pltpu.SemaphoreType.DMA((11,)),
            pltpu.SemaphoreType.DMA((4,)),
        ],
        compiler_params=params,
        cost_estimate=pl.CostEstimate(flops=8 * 10**9, bytes_accessed=8 << 20, transcendentals=0),
        name="mid",
    )(
        levels.reshape(1, 128),
        owner,
        child,
        face_source.reshape(128, 6),
        by_field,
        tables["deriv_0"],
        tables["deriv_1"],
        tables["deriv_2"],
        table,
        large,
        tables["both"],
        flux_jac,
    )
    edge = tables["edge"]

    def post(*refs):
        post_kernel(*refs[:14], edge, *refs[14:])

    result = pl.pallas_call(
        post,
        out_shape=shape((768, 512)),
        in_specs=[HBM] * 12 + [SMEM] * 2,
        out_specs=HBM,
        scratch_shapes=[
            pltpu.VMEM((256, 128), F32),
            pltpu.VMEM((128, 512), F32),
            pltpu.VMEM((128, 384), F32),
            pltpu.VMEM((128, 384), F32),
            pltpu.VMEM((32, 384), F32),
            pltpu.VMEM((768, 288), BF16),
            pltpu.VMEM((768, 384), F32),
            pltpu.VMEM((256, 512), BF16),
            pltpu.VMEM((768, 512), F32),
            pltpu.VMEM((768, 384), F32),
            pltpu.VMEM((768, 128), F32),
            pltpu.VMEM((3, 768, 256), BF16),
            pltpu.VMEM((768, 512), F32),
            pltpu.SemaphoreType.DMA((12,)),
            pltpu.SemaphoreType.DMA((3,)),
        ],
        compiler_params=params,
        cost_estimate=pl.CostEstimate(flops=2 * 10**9, bytes_accessed=4 << 20, transcendentals=0),
        name="post",
    )(
        got.reshape(256, 128),
        tables["project"],
        *arrived,
        small,
        own_back,
        remote,
        local,
        tables["lift"],
        minus_volume,
        flux_jac,
        penalty,
    )
    return result.reshape(6, 128, 512).transpose(1, 0, 2)


def solution(mesh):
    in_specs = (
        P(("gx", "gy"), None, None),
        P(("gx", "gy")),
        P(("gx", "gy")),
        P(("gx", "gy"), None, None),
        P(("gx", "gy"), None, None),
        P(("gx", "gy"), None, None),
        P(),
        P(),
    )
    out_specs = P(("gx", "gy"), None, None)
    return jax.shard_map(
        per_device, mesh=mesh, in_specs=in_specs, out_specs=out_specs, check_vma=False
    )
```

time: 70.7 us -> 58 us (0.82)
  local copies, waits for them, and re-layouts: 19.6 us -> 1.43 us
  Pallas kernels: 17.9 us -> 23.9 us
    unnamed x62 -> x12, local copies, waits for them, and re-layouts: 19.5 us -> 0.66 us
    pallas_call x1, Pallas kernels: 2.74 us -> 5.8 us  [per_device(): pl.pallas_call(pre_kernel, out_shape=[shape((32, 384))] * 4 + [shape((256...]
    pallas_call x1, Pallas kernels: 4.76 us -> 6.72 us  [per_device(): pl.pallas_call(post, out_shape=shape((768, 512)), in_specs=[HBM] * 12 + [...]
    pallas_call x1, Pallas kernels: 10.4 us -> 11.4 us  [per_device(): pl.pallas_call(mid_kernel, out_shape=[shape((768, 384)), shape((768, 288)...]
  transfers between devices with their start and end apart: 5 -> 5, of which waited for: 0 -> 0; matrix products, arithmetic and copies ran while one was open for 0% -> 1% of each run, Pallas kernels for 15% -> 20%
where the time goes in v2:
time: 58 us; the launch traced here: 57.6 us
  starting transfers between devices  32.1 us (55%)
  Pallas kernels  23.9 us (41%)
  local copies, waits for them, and re-layouts  1.43 us (2%)
    ppermute x4, starting transfers between devices, shifted(): return lax.ppermute(value, axis, pairs)  21.9 us
    pallas_call x1, Pallas kernels, per_device(): pl.pallas_call(mid_kernel, out_shape=[shape((768, 384)), shape((768, 288)...  11.4 us
    all_to_all x1, starting transfers between devices, per_device(): lax.all_to_all(mort.reshape(32, 8, 128), 'gy', split_axis=0, concat_axis=...  10.2 us
    pallas_call x1, Pallas kernels, per_device(): pl.pallas_call(post, out_shape=shape((768, 512)), in_specs=[HBM] * 12 + [...  6.72 us
    pallas_call x1, Pallas kernels, per_device(): pl.pallas_call(pre_kernel, out_shape=[shape((32, 384))] * 4 + [shape((256...  5.8 us
  transfers between devices with their start and end apart: 5, of which 0 were waited for; matrix products, arithmetic and copies ran while one was open for 1% of the time, Pallas kernels for 20%

profile of v2, /device:TPU:8, one launch (start us, length us, event | category | flops | bytes accessed | tf_op | source)
XLA Modules:
  0.0 57.6 jit_solution(9511471267031951108)
XLA Ops:
  0.0 5.8 %pre.1 = (f32[32,384]{1,0:T(8,128)}, f32[32,384]{1,0:T(8,128)}, f32[32,384]{1,0:T(8,128)}, f32[32,384]{1,0:T(8,128)}, f32[256,128]{1,0:T(8,128)}, /*index=5*/bf1...) custom-call(f32[768,512]{1,0:T(8,128)} %bitcast.16, s32[4,32]{1,0:T(4,128)} %bitcast.18, s32[1,32]{1,0:T(1,128)} %bitcast.21, ...), custom_call_target="tpu_custom_call" | custom-call | flops 1000000000 | bytes 4194304 | tf_op jit(solution)/shard_map/pre/pallas_call | solution.py:416
  5.8 10.2 %all-to-all-start = ((f32[32,8,128]{2,1,0:T(8,128)}), f32[32,8,128]{2,1,0:T(8,128)S(1)}, u32[]{:S(2)}, u32[]{:S(2)}) async-start(f32[32,8,128]{2,1,0:T(8,128)} %bitcast.15), calls=%async_computation | async-start | bytes 262144 | tf_op jit(solution)/shard_map/all_to_all | solution.py:449
  16.0 14.1 %collective-permute-start = (f32[32,384]{1,0:T(8,128)}, f32[32,384]{1,0:T(8,128)S(1)}, u32[]{:S(2)}, u32[]{:S(2)}) collective-permute-start(f32[32,384]{1,0:T(8,128)} %get-tuple-element.18), channel_id=1, source_target_pairs={{0,510},{1,511},{2,0},{3,1},{4,2},{5,3},{6,4},{7,5},{8,6},{9,7},{1... | collective-permute-start | bytes 147464 | tf_op jit(solution)/shard_map/ppermute | solution.py:26
  30.1 3.4 %collective-permute-start.1 = (f32[32,384]{1,0:T(8,128)}, f32[32,384]{1,0:T(8,128)S(1)}, u32[]{:S(2)}, u32[]{:S(2)}) collective-permute-start(f32[32,384]{1,0:T(8,128)} %get-tuple-element.19), channel_id=1, source_target_pairs={{0,511},{1,0},{2,1},{3,2},{4,3},{5,4},{6,5},{7,6},{8,7},{9,8},{10,... | collective-permute-start | bytes 147464 | tf_op jit(solution)/shard_map/ppermute | solution.py:26
  33.5 2.5 %collective-permute-start.2 = (f32[32,384]{1,0:T(8,128)}, f32[32,384]{1,0:T(8,128)S(1)}, u32[]{:S(2)}, u32[]{:S(2)}) collective-permute-start(f32[32,384]{1,0:T(8,128)} %get-tuple-element.20), channel_id=1, source_target_pairs={{0,1},{1,2},{2,3},{3,4},{4,5},{5,6},{6,7},{7,8},{8,9},{9,10},{10,1... | collective-permute-start | bytes 147464 | tf_op jit(solution)/shard_map/ppermute | solution.py:26
  36.0 1.9 %collective-permute-start.3 = (f32[32,384]{1,0:T(8,128)}, f32[32,384]{1,0:T(8,128)S(1)}, u32[]{:S(2)}, u32[]{:S(2)}) collective-permute-start(f32[32,384]{1,0:T(8,128)} %get-tuple-element.21), channel_id=1, source_target_pairs={{0,2},{1,3},{2,4},{3,5},{4,6},{5,7},{6,8},{7,9},{8,10},{9,11},{10,... | collective-permute-start | bytes 147464 | tf_op jit(solution)/shard_map/ppermute | solution.py:26
  37.9 0.0 copy-done.1
  37.9 0.8 %reshape.34.source_far = s32[128,6]{1,0:T(8,128)} reshape(s32[768]{0:T(1024)S(1)} %copy-done.1) | data formatting | bytes 6144 | tf_op jit(solution)/shard_map/reshape | solution.py:490
  38.7 11.4 %mid.1 = (f32[768,384]{1,0:T(8,128)}, bf16[768,288]{1,0:T(8,128)(2,1)}, f32[32,384]{1,0:T(8,128)}, f32[768,512]{1,0:T(8,128)}) custom-call(s32[1,128]{1,0:T(1,128)} %bitcast.23, s32[1,32]{1,0:T(1,128)} %bitcast.22, s32[4,32]{1,0:T(4,128)} %bitcast.20, s32[128,6]{1,0:T(8,128)} %reshape.34.source_far, f32[768,512]{1,0:T(8,128)} %bitcast.17, ...), custom_call_target="tpu_custom_call" | custom-call | flops 8000000000 | bytes 8388608 | tf_op jit(solution)/shard_map/mid/pallas_call | solution.py:450
  50.1 0.0 collective-permute-done.refs_2_
  50.1 0.0 copy-start.2
  50.1 0.0 collective-permute-done.1.refs_3_
  50.1 0.0 copy-start.3
  50.1 0.0 collective-permute-done.2.refs_4_
  50.1 0.0 copy-start.4
  50.1 0.0 collective-permute-done.3.refs_5_
  50.2 0.0 all-to-all-done
  50.2 0.0 copy-start
  50.2 0.5 copy-done.2
  50.7 0.0 copy-done.3
  50.7 0.0 copy-done.4
  50.8 0.0 copy-done.5
  50.8 0.1 copy-done
  50.8 6.7 %post.1 = f32[768,512]{1,0:T(8,128)} custom-call(f32[256,128]{1,0:T(8,128)} %bitcast.14, f32[128,512]{1,0:T(8,128)} %constant.22.clone.refs_1_, f32[32,384]{1,0:T(8,128)} %copy-done.2, f32[32,384]{1,0:T(8,128)} %copy-done.3, f32[32,384]{1,0:T(8,128)} %copy-done.4, f32[32,384]{1,0:T(8,128)} %copy-done.5, f32[128,384]{1,0:T(8,128)} %get-tuple-element.22.refs_6_, ...), custom_call_target="tpu_custom_call" | custom-call | flops 2000000000 | bytes 4194304 | tf_op jit(solution)/shard_map/post/pallas_call | solution.py:505
  (2 shorter events, 0.0 us)
Async XLA Ops:
  0.0 37.9 %copy-start.1 = (s32[768]{0:T(1024)S(1)}, s32[768]{0:T(1024)}, u32[]{:S(2)}) copy-start(s32[768]{0:T(1024)} %param.18) | copy-start | bytes 9220
  5.8 44.4 %all-to-all-start = ((f32[32,8,128]{2,1,0:T(8,128)}), f32[32,8,128]{2,1,0:T(8,128)S(1)}, u32[]{:S(2)}, u32[]{:S(2)}) async-start(f32[32,8,128]{2,1,0:T(8,128)} %bitcast.15), calls=%async_computation | async-start | bytes 262144 | tf_op jit(solution)/shard_map/all_to_all | solution.py:449
  16.0 34.1 %collective-permute-start = (f32[32,384]{1,0:T(8,128)}, f32[32,384]{1,0:T(8,128)S(1)}, u32[]{:S(2)}, u32[]{:S(2)}) collective-permute-start(f32[32,384]{1,0:T(8,128)} %get-tuple-element.18), channel_id=1, source_target_pairs={{0,510},{1,511},{2,0},{3,1},{4,2},{5,3},{6,4},{7,5},{8,6},{9,7},{1... | collective-permute-start | bytes 147464 | tf_op jit(solution)/shard_map/ppermute | solution.py:26
  30.1 20.0 %collective-permute-start.1 = (f32[32,384]{1,0:T(8,128)}, f32[32,384]{1,0:T(8,128)S(1)}, u32[]{:S(2)}, u32[]{:S(2)}) collective-permute-start(f32[32,384]{1,0:T(8,128)} %get-tuple-element.19), channel_id=1, source_target_pairs={{0,511},{1,0},{2,1},{3,2},{4,3},{5,4},{6,5},{7,6},{8,7},{9,8},{10,... | collective-permute-start | bytes 147464 | tf_op jit(solution)/shard_map/ppermute | solution.py:26
  33.5 16.6 %collective-permute-start.2 = (f32[32,384]{1,0:T(8,128)}, f32[32,384]{1,0:T(8,128)S(1)}, u32[]{:S(2)}, u32[]{:S(2)}) collective-permute-start(f32[32,384]{1,0:T(8,128)} %get-tuple-element.20), channel_id=1, source_target_pairs={{0,1},{1,2},{2,3},{3,4},{4,5},{5,6},{6,7},{7,8},{8,9},{9,10},{10,1... | collective-permute-start | bytes 147464 | tf_op jit(solution)/shard_map/ppermute | solution.py:26
  36.0 14.2 %collective-permute-start.3 = (f32[32,384]{1,0:T(8,128)}, f32[32,384]{1,0:T(8,128)S(1)}, u32[]{:S(2)}, u32[]{:S(2)}) collective-permute-start(f32[32,384]{1,0:T(8,128)} %get-tuple-element.21), channel_id=1, source_target_pairs={{0,2},{1,3},{2,4},{3,5},{4,6},{5,7},{6,8},{7,9},{8,10},{9,11},{10,... | collective-permute-start | bytes 147464 | tf_op jit(solution)/shard_map/ppermute | solution.py:26
  50.1 0.6 %copy-start.2 = (f32[32,384]{1,0:T(8,128)}, f32[32,384]{1,0:T(8,128)S(1)}, u32[]{:S(2)}) copy-start(f32[32,384]{1,0:T(8,128)S(1)} %collective-permute-done.refs_2_) | copy-start | bytes 147460
  50.1 0.6 %copy-start.3 = (f32[32,384]{1,0:T(8,128)}, f32[32,384]{1,0:T(8,128)S(1)}, u32[]{:S(2)}) copy-start(f32[32,384]{1,0:T(8,128)S(1)} %collective-permute-done.1.refs_3_) | copy-start | bytes 147460
  50.1 0.6 %copy-start.4 = (f32[32,384]{1,0:T(8,128)}, f32[32,384]{1,0:T(8,128)S(1)}, u32[]{:S(2)}) copy-start(f32[32,384]{1,0:T(8,128)S(1)} %collective-permute-done.2.refs_4_) | copy-start | bytes 147460
  50.2 0.6 %copy-start.5 = (f32[32,384]{1,0:T(8,128)}, f32[32,384]{1,0:T(8,128)S(1)}, u32[]{:S(2)}) copy-start(f32[32,384]{1,0:T(8,128)S(1)} %collective-permute-done.3.refs_5_) | copy-start | bytes 147460
  50.2 0.7 %copy-start = (f32[32,8,128]{2,1,0:T(8,128)}, f32[32,8,128]{2,1,0:T(8,128)S(1)}, u32[]{:S(2)}) copy-start(f32[32,8,128]{2,1,0:T(8,128)S(1)} %all-to-all-done) | copy-start | bytes 393220

commit v3 on v2

v3 whole, which is shorter than its diff:
```python
import jax
import jax.numpy as jnp
import ml_dtypes
import numpy as np
from jax import lax
from jax.experimental import pallas as pl
from jax.experimental.pallas import tpu as pltpu
from jax.sharding import PartitionSpec as P

P_SIZE = 7
OFFSETS = (-2, -1, 1, 2)
STEP_SIZE = 0.01

F32 = jnp.float32
BF16 = jnp.bfloat16
HIGHEST = lax.Precision.HIGHEST
VMEM = pl.BlockSpec(memory_space=pltpu.VMEM)
HBM = pl.BlockSpec(memory_space=pltpu.HBM)
MIB = 1 << 20


def shifted(value, axis, steps):
    count = lax.axis_size(axis)
    pairs = [(source, (source + steps) % count) for source in range(count)]
    return lax.ppermute(value, axis, pairs)


def pieces_of(table):
    rest = np.asarray(table, np.float32)
    out = []
    for _ in range(2):
        piece = rest.astype(ml_dtypes.bfloat16)
        out.append(piece)
        rest = rest - piece.astype(np.float32)
    return np.stack(out)


def basis_tables(order):
    per_dim = order + 1
    eye_small = np.eye(per_dim)
    points = -np.cos(np.pi * np.arange(per_dim) / order)
    differences = points[:, None] - points[None, :] + eye_small
    barycentric = 1.0 / np.prod(differences, axis=1)
    derivative = barycentric[None, :] / barycentric[:, None] / differences
    derivative = np.where(eye_small > 0, 0.0, derivative)
    derivative = derivative - eye_small * derivative.sum(axis=1)[:, None]
    angles = np.pi * np.arange(per_dim) / order
    weights = np.ones(per_dim)
    for wave in range(1, order // 2 + 1):
        factor = 1.0 if 2 * wave == order else 2.0
        weights = weights - factor * np.cos(2.0 * wave * angles) / (4.0 * wave * wave - 1.0)
    edge_factor = np.where((np.arange(per_dim) == 0) | (np.arange(per_dim) == order), 1.0, 2.0)
    weights = edge_factor * weights / order

    def lagrange(targets):
        values_at = np.ones((per_dim, per_dim))
        for column in range(per_dim):
            for other in range(per_dim):
                if other != column:
                    values_at[:, column] *= (targets - points[other]) / (
                        points[column] - points[other]
                    )
        return values_at

    halves = [lagrange((points - 1.0) / 2.0), lagrange((points + 1.0) / 2.0)]
    identity = np.eye(per_dim)
    node_index = np.arange(per_dim**3).reshape(per_dim, per_dim, per_dim)
    fnodes = per_dim * per_dim
    select = np.zeros((per_dim**3, 4 * fnodes), np.float32)
    for face in range(2, 6):
        picker = [slice(None), slice(None), slice(None)]
        picker[face // 2] = 0 if face % 2 == 0 else order
        on_face = node_index[tuple(picker)].reshape(-1)
        select[on_face, (face - 2) * fnodes + np.arange(fnodes)] = 1.0
    face_weight = np.kron(weights, weights)
    proj = [np.kron(halves[quad // 2], halves[quad % 2]) for quad in range(4)]
    restrict = [
        0.25 * (proj[quad].T * face_weight[None, :]) / face_weight[:, None] for quad in range(4)
    ]
    two = np.eye(2)
    both = sum(restrict[quad] @ proj[quad] for quad in range(4))
    quarter = np.eye(4)
    return {
        "select": select.astype(ml_dtypes.bfloat16),
        "lift": np.concatenate([select.T, select.T], 0).astype(ml_dtypes.bfloat16),
        "restrict": np.concatenate([np.kron(two, r.T) for r in restrict], 0).astype(np.float32),
        "project": np.concatenate([np.kron(two, p.T) for p in proj], 1).astype(np.float32),
        "both": np.kron(two, both.T).astype(np.float32),
        "deriv_0": pieces_of(np.kron(derivative, np.eye(fnodes)).T),
        "deriv_1": pieces_of(np.kron(quarter, np.kron(derivative, identity)).T),
        "deriv_2": pieces_of(np.kron(quarter, np.kron(identity, derivative)).T),
        "edge": float(1.0 / weights[0]),
    }


def split3(value):
    high = value.astype(BF16)
    rest = value - high.astype(F32)
    middle = rest.astype(BF16)
    low = (rest - middle.astype(F32)).astype(BF16)
    return high, middle, low


def mm(a, b):
    return jnp.dot(a, b, preferred_element_type=F32)


def low_half(rows):
    return lax.broadcasted_iota(jnp.int32, (rows, 128), 1) < 64


def swap_halves(value):
    return pltpu.roll(value, 64, 1)


def column_of(row):
    count = row.shape[1]
    spread = jnp.broadcast_to(row.astype(F32), (count, count))
    down = lax.broadcasted_iota(jnp.int32, (count, count), 0)
    across = lax.broadcasted_iota(jnp.int32, (count, count), 1)
    return jnp.sum(jnp.where(down == across, spread, 0.0), axis=1, keepdims=True).astype(jnp.int32)


def start_all(sources, targets, arrivals):
    copies = [
        pltpu.make_async_copy(source, target, arrivals.at[at])
        for at, (source, target) in enumerate(zip(sources, targets, strict=True))
    ]
    for copy in copies:
        copy.start()
    return copies


def rows_of(field):
    return slice(128 * field, 128 * field + 128)


def slot_or_spare(slot):
    return jnp.where(slot < 0, 768, slot)


def pre_kernel(
    state_far, send_far, owner_far, child_far, select_far, restrict_far,
    s0_far, s1_far, s2_far, s3_far, mort_far, table_far, large_far,
    state, send, owner, child, select, restrict, pieces, table, picked, mort, arrivals, sent,
):
    copies = start_all(
        [*(state_far.at[rows_of(f)] for f in range(6)), select_far, send_far, owner_far, child_far, restrict_far],
        [*(state.at[rows_of(f)] for f in range(6)), select, send, owner, child, restrict],
        arrivals,
    )
    low = low_half(128)
    table[:, 768:776] = jnp.zeros((3, 8, 128), F32)
    for part in (6, 7):
        mort[pl.ds(part, 32, stride=8), :] = jnp.zeros((32, 128), F32)
    for field in range(6):
        copies[field].wait()
        for piece, value in enumerate(split3(state[rows_of(field)])):
            pieces[piece, rows_of(field)] = value
    copies[6].wait()
    inner = (
        mm(pieces[0], select[...]) + mm(pieces[1], select[...]) + mm(pieces[2], select[...])
    )
    for pair in range(3):
        even, odd = rows_of(2 * pair), rows_of(2 * pair + 1)
        fronts = [(state[even, :128], state[odd, :128])]
        backs = [(state[even, 384:], state[odd, 384:])]
        for dim in range(2):
            at = slice(128 * dim, 128 * dim + 128)
            fronts.append((inner[even, at], inner[odd, at]))
        backs += fronts[1:]
        for dim in range(3):
            front = jnp.where(low, fronts[dim][0], swap_halves(fronts[dim][1]))
            back = jnp.where(low, swap_halves(backs[dim][0]), backs[dim][1])
            table[pair, pl.ds(2 * dim, 128, stride=6), :] = front
            table[pair, pl.ds(2 * dim + 1, 128, stride=6), :] = back
    leaving = start_all([table.at[:, 0:768]], [table_far], sent)
    for copy in copies[7:]:
        copy.wait()

    def move(out, row, slot):
        for pair in range(3):
            out[row : row + 1, 128 * pair : 128 * pair + 128] = table[pair, pl.ds(slot, 1), :]

    for q in range(4):
        for at in range(32):
            move(picked, 32 + 32 * q + at, slot_or_spare(child[q, at]))
    for at in range(32):
        move(picked, at, slot_or_spare(owner[0, at]))
    for o, out in enumerate((s0_far, s1_far, s2_far, s3_far)):
        for at in range(32):
            move(picked, 160 + 32 * o + at, send[o, at])
        leaving += start_all([picked.at[160 + 32 * o : 192 + 32 * o]], [out], sent.at[2 + o : 3 + o])
    leaving += start_all([picked.at[0:32]], [large_far], sent.at[1:2])
    for part in range(3):
        mort[pl.ds(3 + part, 32, stride=8), :] = picked[0:32, 128 * part : 128 * part + 128]
    stacked = jnp.concatenate(
        [
            jnp.concatenate(
                [
                    picked[32 + 32 * q : 64 + 32 * q, 128 * part : 128 * part + 128]
                    for q in range(4)
                ],
                1,
            )
            for part in range(3)
        ],
        0,
    )
    back = jnp.dot(stacked, restrict[...], precision=HIGHEST, preferred_element_type=F32)
    for part in range(3):
        mort[pl.ds(part, 32, stride=8), :] = back[32 * part : 32 * part + 32]
    leaving += start_all([mort], [mort_far], sent.at[6:7])
    for copy in leaving:
        copy.wait()


def wanted_column(sources, face):
    down = lax.broadcasted_iota(jnp.int32, (128, 128), 0)
    across = lax.broadcasted_iota(jnp.int32, (128, 128), 1)
    spread = jnp.zeros((128, 128), F32)
    for part in range(6):
        hit = across + 128 * part == 6 * down + face
        spread = jnp.where(hit, sources[part : part + 1], spread)
    return jnp.sum(spread, axis=1, keepdims=True).astype(jnp.int32)


def add_owned(jumps, owner, levels, rows, sign):
    for at in range(32):
        slot = owner[0, at]
        element = jnp.where(slot < 0, 0, (slot * 10923) >> 16)
        scale = sign * (1 << levels[0, element]).astype(F32)
        row = (slot - 6 * element) * 128 + element
        target = pl.ds(jnp.where(slot < 0, 768, row), 1)
        jumps[target] = jumps[target] + scale * rows[at : at + 1]


def by_field_order(jumps, values):
    low = low_half(128)
    for dim in range(3):
        at = slice(128 * dim, 128 * dim + 128)
        for pair in range(3):
            lanes = slice(128 * pair, 128 * pair + 128)
            front = jumps[256 * dim : 256 * dim + 128, lanes]
            back = jumps[256 * dim + 128 : 256 * dim + 256, lanes]
            values[rows_of(2 * pair), at] = jnp.where(low, front, swap_halves(back))
            values[rows_of(2 * pair + 1), at] = jnp.where(low, swap_halves(front), back)


def add_surface(values, flux, penalty, factor, surfaces, lift, out, out_far, ready, done):
    step = 32
    low = low_half(step)
    signs = jnp.where(low, -factor, factor)
    sent = []
    for pair in range(3):
        rows = slice(256 * pair, 256 * pair + 256)
        ready(pair)
        for field in (2 * pair, 2 * pair + 1):
            drag = factor * penalty[field]
            for dim in range(3):
                lanes = slice(128 * dim, 128 * dim + 128)
                rates = [flux[dim, field, other] for other in range(6)]
                for first in range(0, 128, step):
                    mixed = rates[0] * values[first : first + step, lanes]
                    for other in range(1, 6):
                        at = 128 * other + first
                        mixed = mixed + rates[other] * values[at : at + step, lanes]
                    at = 128 * field + first
                    surface = signs * mixed - drag * values[at : at + step, lanes]
                    if dim == 0:
                        out[at : at + step, 0:128] += jnp.where(low, surface, 0.0)
                        out[at : at + step, 384:512] += jnp.where(low, 0.0, surface)
                    else:
                        high = surface.astype(BF16)
                        surfaces[at : at + step, 128 * dim - 128 : 128 * dim] = high
                        rest = (surface - high.astype(F32)).astype(BF16)
                        surfaces[at : at + step, 128 * dim + 128 : 128 * dim + 256] = rest
        out[rows] += mm(surfaces[rows], lift[...])
        copy = pltpu.make_async_copy(out.at[rows], out_far.at[rows], done.at[pair])
        copy.start()
        sent.append(copy)
    return sent


def mid_kernel(
    levels_far, child_far, source_far, flux_far, penalty_far, owner_far, state_far, d0_far, d1_far,
    d2_far, table_far, large_far, both_far, lift_far, edge, out_far,
    levels, child, source, flux, penalty, owner, levels_near, state, d0, d1, d2, table, large, both,
    lift, out, pieces, grads, matrix, amount, traces, jumps, values, surfaces,
    arrivals, sent,
):
    copies = start_all(
        [levels_far, child_far, source_far], [levels, child, source], arrivals.at[0:3]
    )
    state_copies = start_all(
        [state_far.at[rows_of(f)] for f in range(6)],
        [state.at[rows_of(f)] for f in range(6)],
        arrivals.at[3:9],
    )
    copies += [None] + start_all(
        [flux_far, penalty_far, d0_far, d1_far, d2_far, owner_far, levels_far],
        [flux, penalty, d0, d1, d2, owner, levels_near],
        arrivals.at[9:16],
    )
    for copy in copies[:3]:
        copy.wait()
    level = column_of(levels[...])
    twos = (1 << level).astype(F32)
    minus = -twos
    amount[...] = jnp.broadcast_to(minus * STEP_SIZE, (128, 128))
    slots = lax.broadcasted_iota(jnp.int32, (1, 768), 1)
    element = lax.broadcasted_iota(jnp.int32, (128, 1), 0)
    child_row = jnp.concatenate([child[q : q + 1, :] for q in range(4)], 1)
    sources = source[...].astype(F32)
    for face in range(6):
        wanted = wanted_column(sources, face)
        mine = 6 * element + face
        rows = rows_of(face)
        as_child = jnp.where(mine == child_row, twos, 0.0)
        own = jnp.where(wanted >= 0, twos, 0.0) + jnp.sum(as_child, axis=1, keepdims=True)
        for other in range(6):
            at = slots[:, rows_of(other)]
            block = jnp.where(wanted == at, minus, 0.0) + jnp.where(mine == at, own, 0.0)
            matrix[rows, rows_of(other)] = block.astype(BF16)
    for field in range(6):
        state_copies[field].wait()
        rows = rows_of(field)
        value = state[rows]
        high = value.astype(BF16)
        pieces[0, rows] = high
        pieces[1, rows] = (value - high.astype(F32)).astype(BF16)
    later = start_all(
        [table_far, large_far, both_far, lift_far], [table, large, both, lift], arrivals.at[17:21]
    )
    for copy in copies[6:9]:
        copy.wait()

    def apply(lanes, deriv):
        high, rest = pieces[0, :, lanes], pieces[1, :, lanes]
        return mm(high, deriv[0]) + (mm(high, deriv[1]) + mm(rest, deriv[0]))

    grads[0] = apply(slice(0, 512), d0)
    for half in range(2):
        lanes = slice(256 * half, 256 * half + 256)
        grads[1, :, lanes] = apply(lanes, d1)
        grads[2, :, lanes] = apply(lanes, d2)
    for copy in later + copies[4:6]:
        copy.wait()
    for first in range(0, 128, 16):
        scale = amount[first : first + 16]
        scale = jnp.concatenate([scale] * 4, 1)
        for field in range(6):
            total = None
            for dim in range(3):
                for other in range(6):
                    rows = slice(128 * other + first, 128 * other + first + 16)
                    term = flux[dim, field, other] * grads[dim, rows, :]
                    total = term if total is None else total + term
            out[128 * field + first : 128 * field + first + 16] = scale * total
    for pair in range(3):
        for piece, value in enumerate(split3(table[pair])):
            first = 384 * piece + 128 * pair
            traces[:, first : first + 128] = value
    back = jnp.concatenate(
        [
            jnp.dot(
                large[:, 128 * part : 128 * part + 128],
                both[...],
                precision=HIGHEST,
                preferred_element_type=F32,
            )
            for part in range(3)
        ],
        1,
    )
    total = mm(matrix[...], traces[...])
    jumps[0:768] = total[:, 0:384] + total[:, 384:768] + total[:, 768:1152]
    copies[9].wait()
    copies[10].wait()
    add_owned(jumps, owner, levels_near, back, 1.0)
    by_field_order(jumps, values)
    leaving = add_surface(
        values, flux, penalty, 0.5 * STEP_SIZE * edge, surfaces, lift, out, out_far,
        lambda pair: None, sent,
    )
    for copy in leaving:
        copy.wait()


def post_kernel(
    got, a0, a1, a2, a3, project, source, child, levels_row, flux_far, penalty_far, owner_far,
    levels_far, lift_far, local_far, edge, out_far,
    flux, penalty, owner, levels, lift, out, remote, extra, jumps, values, surfaces,
    arrivals, done,
):
    thirds = [slice(256 * pair, 256 * pair + 256) for pair in range(3)]
    copies = start_all(
        [flux_far, penalty_far, owner_far, levels_far, lift_far, *(local_far.at[rows] for rows in thirds)],
        [flux, penalty, owner, levels, lift, *(out.at[rows] for rows in thirds)],
        arrivals,
    )
    minus = -(1 << column_of(levels_row[...])).astype(F32)
    element = lax.broadcasted_iota(jnp.int32, (128, 1), 0)
    arrived_slot = 768 + lax.broadcasted_iota(jnp.int32, (1, 128), 1)
    child_row = jnp.concatenate([child[q : q + 1, :] for q in range(4)], 1)
    sources = source[...].astype(F32)
    for face in range(6):
        wanted, mine = wanted_column(sources, face), 6 * element + face
        remote[rows_of(face), 0:128] = jnp.where(wanted == arrived_slot, minus, 0.0).astype(BF16)
        remote[rows_of(face), 128:256] = jnp.where(mine == child_row, minus, 0.0).astype(BF16)
    for place, rows in enumerate((a0, a1, a2, a3)):
        for piece, value in enumerate(split3(rows[...])):
            extra[32 * place : 32 * place + 32, 384 * piece : 384 * piece + 384] = value
    got_back = [got[pl.ds(part, 32, stride=8), :] for part in range(3)]
    got_large = [got[pl.ds(3 + part, 32, stride=8), :] for part in range(3)]
    onto = jnp.dot(
        jnp.concatenate(got_large, 0), project[...], precision=HIGHEST, preferred_element_type=F32
    )
    for piece, value in enumerate(split3(onto)):
        for part in range(3):
            lanes = slice(384 * piece + 128 * part, 384 * piece + 128 * part + 128)
            for q in range(4):
                extra[128 + 32 * q : 160 + 32 * q, lanes] = value[
                    32 * part : 32 * part + 32, 128 * q : 128 * q + 128
                ]
    total = mm(remote[...], extra[...])
    jumps[0:768] = total[:, 0:384] + total[:, 384:768] + total[:, 768:1152]
    for copy in copies[:5]:
        copy.wait()
    add_owned(jumps, owner, levels, jnp.concatenate(got_back, 1), -1.0)
    by_field_order(jumps, values)
    sent = add_surface(
        values, flux, penalty, 0.5 * STEP_SIZE * edge, surfaces, lift, out, out_far,
        lambda pair: copies[5 + pair].wait(), done,
    )
    for copy in sent:
        copy.wait()


def per_device(state, levels, face_source, face_send, mort_owner, mort_child, flux_jac, penalty):
    tables = basis_tables(P_SIZE)
    by_field = state.transpose(1, 0, 2).reshape(768, 512)
    send = face_send.reshape(4, 32)
    owner = mort_owner.reshape(1, 32)
    child = mort_child.transpose(0, 2, 1).reshape(4, 32)

    def shape(dims, kind=F32):
        return jax.ShapeDtypeStruct(dims, kind)

    def params(mib):
        return pltpu.CompilerParams(vmem_limit_bytes=mib * MIB)

    s0, s1, s2, s3, mort, table, large = pl.pallas_call(
        pre_kernel,
        out_shape=[shape((32, 384))] * 4
        + [shape((256, 128)), shape((3, 768, 128)), shape((32, 384))],
        in_specs=[HBM] * 6,
        out_specs=[HBM] * 7,
        scratch_shapes=[
            pltpu.VMEM((768, 512), F32),
            pltpu.SMEM((4, 32), jnp.int32),
            pltpu.SMEM((1, 32), jnp.int32),
            pltpu.SMEM((4, 32), jnp.int32),
            pltpu.VMEM((512, 256), BF16),
            pltpu.VMEM((512, 128), F32),
            pltpu.VMEM((3, 768, 512), BF16),
            pltpu.VMEM((3, 776, 128), F32),
            pltpu.VMEM((288, 384), F32),
            pltpu.VMEM((256, 128), F32),
            pltpu.SemaphoreType.DMA((11,)),
            pltpu.SemaphoreType.DMA((7,)),
        ],
        compiler_params=params(60),
        cost_estimate=pl.CostEstimate(flops=10**9, bytes_accessed=4 << 20, transcendentals=0),
        name="pre",
    )(by_field, send, owner, child, tables["select"], tables["restrict"])
    arrived = [
        shifted(rows, ("gx", "gy"), OFFSETS[place]) for place, rows in enumerate((s0, s1, s2, s3))
    ]
    got = lax.all_to_all(mort.reshape(32, 8, 128), "gy", split_axis=0, concat_axis=0, tiled=True)
    edge = tables["edge"]

    def mid(*refs):
        mid_kernel(*refs[:14], edge, *refs[14:])

    local = pl.pallas_call(
        mid,
        out_shape=shape((768, 512)),
        in_specs=[HBM] * 14,
        out_specs=HBM,
        scratch_shapes=[
            pltpu.VMEM((1, 128), jnp.int32),
            pltpu.VMEM((4, 32), jnp.int32),
            pltpu.VMEM((6, 128), jnp.int32),
            pltpu.SMEM((3, 6, 6), F32),
            pltpu.SMEM((6,), F32),
            pltpu.SMEM((1, 32), jnp.int32),
            pltpu.SMEM((1, 128), jnp.int32),
            pltpu.VMEM((768, 512), F32),
            pltpu.VMEM((2, 512, 512), BF16),
            pltpu.VMEM((2, 256, 256), BF16),
            pltpu.VMEM((2, 256, 256), BF16),
            pltpu.VMEM((3, 768, 128), F32),
            pltpu.VMEM((32, 384), F32),
            pltpu.VMEM((128, 128), F32),
            pltpu.VMEM((512, 512), BF16),
            pltpu.VMEM((768, 512), F32),
            pltpu.VMEM((2, 768, 512), BF16),
            pltpu.VMEM((3, 768, 512), F32),
            pltpu.VMEM((768, 768), BF16),
            pltpu.VMEM((128, 128), F32),
            pltpu.VMEM((768, 1152), BF16),
            pltpu.VMEM((776, 384), F32),
            pltpu.VMEM((768, 384), F32),
            pltpu.VMEM((768, 512), BF16),
            pltpu.SemaphoreType.DMA((21,)),
            pltpu.SemaphoreType.DMA((3,)),
        ],
        compiler_params=params(60),
        cost_estimate=pl.CostEstimate(flops=8 * 10**9, bytes_accessed=8 << 20, transcendentals=0),
        name="mid",
    )(
        levels.reshape(1, 128),
        child,
        face_source.reshape(6, 128),
        flux_jac,
        penalty,
        owner,
        by_field,
        tables["deriv_0"],
        tables["deriv_1"],
        tables["deriv_2"],
        table,
        large,
        tables["both"],
        tables["lift"],
    )

    def post(*refs):
        post_kernel(*refs[:15], edge, *refs[15:])

    result = pl.pallas_call(
        post,
        out_shape=shape((768, 512)),
        in_specs=[VMEM] * 9 + [HBM] * 6,
        out_specs=HBM,
        input_output_aliases={14: 0},
        scratch_shapes=[
            pltpu.SMEM((3, 6, 6), F32),
            pltpu.SMEM((6,), F32),
            pltpu.SMEM((1, 32), jnp.int32),
            pltpu.SMEM((1, 128), jnp.int32),
            pltpu.VMEM((512, 512), BF16),
            pltpu.VMEM((768, 512), F32),
            pltpu.VMEM((768, 256), BF16),
            pltpu.VMEM((256, 1152), BF16),
            pltpu.VMEM((776, 384), F32),
            pltpu.VMEM((768, 384), F32),
            pltpu.VMEM((768, 512), BF16),
            pltpu.SemaphoreType.DMA((8,)),
            pltpu.SemaphoreType.DMA((3,)),
        ],
        compiler_params=params(32),
        cost_estimate=pl.CostEstimate(flops=2 * 10**9, bytes_accessed=4 << 20, transcendentals=0),
        name="post",
    )(
        got.reshape(256, 128),
        *arrived,
        tables["project"],
        face_source.reshape(6, 128),
        child,
        levels.reshape(1, 128),
        flux_jac,
        penalty,
        owner,
        levels.reshape(1, 128),
        tables["lift"],
        local,
    )
    return result.reshape(6, 128, 512).transpose(1, 0, 2)


def solution(mesh):
    in_specs = (
        P(("gx", "gy"), None, None),
        P(("gx", "gy")),
        P(("gx", "gy")),
        P(("gx", "gy"), None, None),
        P(("gx", "gy"), None, None),
        P(("gx", "gy"), None, None),
        P(),
        P(),
    )
    out_specs = P(("gx", "gy"), None, None)
    return jax.shard_map(
        per_device, mesh=mesh, in_specs=in_specs, out_specs=out_specs, check_vma=False
    )
```

time: 58 us -> 52.4 us (0.903)
  Pallas kernels: 23.9 us -> 19.4 us
  local copies, waits for them, and re-layouts: 1.43 us -> 0.05 us
    pallas_call x2, Pallas kernels: 18.1 us -> 15.4 us  [the longest x1 11.3 us: per_device(): pl.pallas_call(mid, out_shape=shape((768, 512)), in_specs=[HBM] * 14, out...]
    pallas_call x1, Pallas kernels: 5.8 us -> 4.05 us  [per_device(): pl.pallas_call(pre_kernel, out_shape=[shape((32, 384))] * 4 + [shape((256...]
    reshape x1 -> x0, local copies, waits for them, and re-layouts: 0.77 us -> none  [per_device(): face_source.reshape(128, 6)]
    unnamed x12 -> x16, local copies, waits for them, and re-layouts: 0.66 us -> 0.05 us
  transfers between devices with their start and end apart: 5 -> 5, of which waited for: 0 -> 0; matrix products, arithmetic and copies ran while one was open for 1% -> 0% of each run, Pallas kernels for 20% -> 22%
where the time goes in v3:
time: 52.4 us; the launch traced here: 52.1 us
  starting transfers between devices  32.3 us (62%)
  Pallas kernels  19.4 us (37%)
    ppermute x4, starting transfers between devices, shifted(): return lax.ppermute(value, axis, pairs)  22.1 us
    pallas_call x1, Pallas kernels, per_device(): pl.pallas_call(mid, out_shape=shape((768, 512)), in_specs=[HBM] * 14, out...  11.3 us
    all_to_all x1, starting transfers between devices, per_device(): lax.all_to_all(mort.reshape(32, 8, 128), 'gy', split_axis=0, concat_axis=...  10.2 us
    pallas_call x1, Pallas kernels, per_device(): pl.pallas_call(post, out_shape=shape((768, 512)), in_specs=[VMEM] * 9 + [...  4.12 us
    pallas_call x1, Pallas kernels, per_device(): pl.pallas_call(pre_kernel, out_shape=[shape((32, 384))] * 4 + [shape((256...  4.05 us
  transfers between devices with their start and end apart: 5, of which 0 were waited for; matrix products, arithmetic and copies ran while one was open for 0% of the time, Pallas kernels for 22%

profile of v3, /device:TPU:8, one launch (start us, length us, event | category | flops | bytes accessed | tf_op | source)
XLA Modules:
  0.0 52.1 jit_solution(355383039789965722)
XLA Ops:
  0.0 4.0 %pre.1 = (f32[32,384]{1,0:T(8,128)}, f32[32,384]{1,0:T(8,128)}, f32[32,384]{1,0:T(8,128)}, f32[32,384]{1,0:T(8,128)}, f32[256,128]{1,0:T(8,128)}, /*index=5*/f32[3,768,128]{2,1,0:T(8,128)}, f32[32,384]{1,0:T(8,128)}) custom-call(f32[768,512]{1,0:T(8,128)} %bitcast.28, s32[4,32]{1,0:T(4,128)} %bitcast.30, s32[1,32]{1,0:T(1,128)} %bitcast.21, ...), custom_call_target="tpu_custom_call" | custom-call | flops 1000000000 | bytes 4194304 | tf_op jit(solution)/shard_map/pre/pallas_call | solution.py:453
  4.1 10.2 %all-to-all-start = ((f32[32,8,128]{2,1,0:T(8,128)}), f32[32,8,128]{2,1,0:T(8,128)S(1)}, u32[]{:S(2)}, u32[]{:S(2)}) async-start(f32[32,8,128]{2,1,0:T(8,128)} %bitcast.27), calls=%async_computation | async-start | bytes 262144 | tf_op jit(solution)/shard_map/all_to_all | solution.py:480
  14.2 14.1 %collective-permute-start = (f32[32,384]{1,0:T(8,128)}, f32[32,384]{1,0:T(8,128)S(1)}, u32[]{:S(2)}, u32[]{:S(2)}) collective-permute-start(f32[32,384]{1,0:T(8,128)} %get-tuple-element.13), channel_id=1, source_target_pairs={{0,510},{1,511},{2,0},{3,1},{4,2},{5,3},{6,4},{7,5},{8,6},{9,7},{1... | collective-permute-start | bytes 147464 | tf_op jit(solution)/shard_map/ppermute | solution.py:25
  28.4 3.4 %collective-permute-start.1 = (f32[32,384]{1,0:T(8,128)}, f32[32,384]{1,0:T(8,128)S(1)}, u32[]{:S(2)}, u32[]{:S(2)}) collective-permute-start(f32[32,384]{1,0:T(8,128)} %get-tuple-element.14), channel_id=1, source_target_pairs={{0,511},{1,0},{2,1},{3,2},{4,3},{5,4},{6,5},{7,6},{8,7},{9,8},{10,... | collective-permute-start | bytes 147464 | tf_op jit(solution)/shard_map/ppermute | solution.py:25
  31.8 2.5 %collective-permute-start.2 = (f32[32,384]{1,0:T(8,128)}, f32[32,384]{1,0:T(8,128)S(1)}, u32[]{:S(2)}, u32[]{:S(2)}) collective-permute-start(f32[32,384]{1,0:T(8,128)} %get-tuple-element.15), channel_id=1, source_target_pairs={{0,1},{1,2},{2,3},{3,4},{4,5},{5,6},{6,7},{7,8},{8,9},{9,10},{10,1... | collective-permute-start | bytes 147464 | tf_op jit(solution)/shard_map/ppermute | solution.py:25
  34.2 2.1 %collective-permute-start.3 = (f32[32,384]{1,0:T(8,128)}, f32[32,384]{1,0:T(8,128)S(1)}, u32[]{:S(2)}, u32[]{:S(2)}) collective-permute-start(f32[32,384]{1,0:T(8,128)} %get-tuple-element.16), channel_id=1, source_target_pairs={{0,2},{1,3},{2,4},{3,5},{4,6},{5,7},{6,8},{7,9},{8,10},{9,11},{10,... | collective-permute-start | bytes 147464 | tf_op jit(solution)/shard_map/ppermute | solution.py:25
  36.4 0.0 copy-start
  36.4 0.0 copy-start.1
  36.4 0.0 copy-start.2
  36.4 0.0 copy-start.3
  36.4 0.0 copy-start.4
  36.4 0.0 copy-start.5
  36.4 0.0 copy-start.6
  36.4 0.0 copy-start.7
  36.5 11.3 %mid.1.refs_14_ = f32[768,512]{1,0:T(8,128)} custom-call(s32[1,128]{1,0:T(1,128)} %bitcast.24, s32[4,32]{1,0:T(4,128)} %bitcast.19, s32[6,128]{1,0:T(8,128)} %bitcast.16, f32[3,6,6]{2,1,0:T(8,128)} %refs_9_.2, f32[6]{0:T(128)} %refs_10_.1, s32[1,32]{1,0:T(1,128)} %bitcast.22, f32[768,512]{1,0:T(8,128)} %bitcast.29, ...), custom_call_target="tpu_custom_call" | custom-call | flops 8000000000 | bytes 8388608 | tf_op jit(solution)/shard_map/mid/pallas_call | solution.py:486
  47.7 0.0 collective-permute-done.refs_1_
  47.7 0.0 collective-permute-done.1.refs_2_
  47.7 0.0 collective-permute-done.2.refs_3_
  47.7 0.0 collective-permute-done.3.refs_4_
  47.8 0.0 all-to-all-done
  47.8 0.0 copy-done
  47.8 0.0 copy-done.1
  47.8 0.0 copy-done.2
  47.8 4.1 %post.1 = f32[768,512]{1,0:T(8,128)} custom-call(f32[256,128]{1,0:T(8,128)S(1)} %bitcast.15, f32[32,384]{1,0:T(8,128)S(1)} %collective-permute-done.refs_1_, f32[32,384]{1,0:T(8,128)S(1)} %collective-permute-done.1.refs_2_, f32[32,384]{1,0:T(8,128)S(1)} %collective-permute-done.2.refs_3_, ...), custom_call_target="tpu_custom_call", output_to_operand_aliasing={{}: (14, {})} | custom-call | flops 2000000000 | bytes 4194304 | tf_op jit(solution)/shard_map/post/pallas_call | solution.py:542
  (5 shorter events, 0.0 us)
Async XLA Ops:
  4.1 43.7 %all-to-all-start = ((f32[32,8,128]{2,1,0:T(8,128)}), f32[32,8,128]{2,1,0:T(8,128)S(1)}, u32[]{:S(2)}, u32[]{:S(2)}) async-start(f32[32,8,128]{2,1,0:T(8,128)} %bitcast.27), calls=%async_computation | async-start | bytes 262144 | tf_op jit(solution)/shard_map/all_to_all | solution.py:480
  14.2 33.5 %collective-permute-start = (f32[32,384]{1,0:T(8,128)}, f32[32,384]{1,0:T(8,128)S(1)}, u32[]{:S(2)}, u32[]{:S(2)}) collective-permute-start(f32[32,384]{1,0:T(8,128)} %get-tuple-element.13), channel_id=1, source_target_pairs={{0,510},{1,511},{2,0},{3,1},{4,2},{5,3},{6,4},{7,5},{8,6},{9,7},{1... | collective-permute-start | bytes 147464 | tf_op jit(solution)/shard_map/ppermute | solution.py:25
  28.4 19.3 %collective-permute-start.1 = (f32[32,384]{1,0:T(8,128)}, f32[32,384]{1,0:T(8,128)S(1)}, u32[]{:S(2)}, u32[]{:S(2)}) collective-permute-start(f32[32,384]{1,0:T(8,128)} %get-tuple-element.14), channel_id=1, source_target_pairs={{0,511},{1,0},{2,1},{3,2},{4,3},{5,4},{6,5},{7,6},{8,7},{9,8},{10,... | collective-permute-start | bytes 147464 | tf_op jit(solution)/shard_map/ppermute | solution.py:25
  31.8 16.0 %collective-permute-start.2 = (f32[32,384]{1,0:T(8,128)}, f32[32,384]{1,0:T(8,128)S(1)}, u32[]{:S(2)}, u32[]{:S(2)}) collective-permute-start(f32[32,384]{1,0:T(8,128)} %get-tuple-element.15), channel_id=1, source_target_pairs={{0,1},{1,2},{2,3},{3,4},{4,5},{5,6},{6,7},{7,8},{8,9},{9,10},{10,1... | collective-permute-start | bytes 147464 | tf_op jit(solution)/shard_map/ppermute | solution.py:25
  34.2 13.5 %collective-permute-start.3 = (f32[32,384]{1,0:T(8,128)}, f32[32,384]{1,0:T(8,128)S(1)}, u32[]{:S(2)}, u32[]{:S(2)}) collective-permute-start(f32[32,384]{1,0:T(8,128)} %get-tuple-element.16), channel_id=1, source_target_pairs={{0,2},{1,3},{2,4},{3,5},{4,6},{5,7},{6,8},{7,9},{8,10},{9,11},{10,... | collective-permute-start | bytes 147464 | tf_op jit(solution)/shard_map/ppermute | solution.py:25
  36.4 11.4 %copy-start = (f32[3,6,6]{2,1,0:T(8,128)S(1)}, f32[3,6,6]{2,1,0:T(8,128)}, u32[]{:S(2)}) copy-start(f32[3,6,6]{2,1,0:T(8,128)} %refs_9_.2) | copy-start | bytes 1300
  36.4 11.4 %copy-start.1 = (s32[768]{0:T(1024)S(1)}, s32[768]{0:T(1024)}, u32[]{:S(2)}) copy-start(s32[768]{0:T(1024)} %param.18) | copy-start | bytes 9220
  36.4 11.4 %copy-start.2 = (s32[1,32,4]{1,2,0:T(4,128)S(1)}, s32[1,32,4]{1,2,0:T(4,128)}, u32[]{:S(2)}) copy-start(s32[1,32,4]{1,2,0:T(4,128)} %param.21) | copy-start | bytes 1540
  36.4 11.4 %copy-start.3 = (s32[1,32,1]{1,2,0:T(1,128)S(1)}, s32[1,32,1]{1,2,0:T(1,128)}, u32[]{:S(2)}) copy-start(s32[1,32,1]{1,2,0:T(1,128)} %param.20) | copy-start | bytes 388
  36.4 11.4 %copy-start.4 = (s32[128]{0:T(128)S(1)}, s32[128]{0:T(128)}, u32[]{:S(2)}) copy-start(s32[128]{0:T(128)} %param.17) | copy-start | bytes 1540
  36.4 11.4 %copy-start.5 = (f32[6]{0:T(128)S(1)}, f32[6]{0:T(128)}, u32[]{:S(2)}) copy-start(f32[6]{0:T(128)} %refs_10_.1) | copy-start | bytes 76
  36.4 11.4 %copy-start.6 = (bf16[512,512]{1,0:T(8,128)(2,1)S(1)}, bf16[512,512]{1,0:T(8,128)(2,1)}, u32[]{:S(2)}) copy-start(bf16[512,512]{1,0:T(8,128)(2,1)} %constant.22.clone.refs_13_) | copy-start | bytes 1572868
  36.4 11.4 %copy-start.7 = (f32[128,512]{1,0:T(8,128)S(1)}, f32[128,512]{1,0:T(8,128)}, u32[]{:S(2)}) copy-start(f32[128,512]{1,0:T(8,128)} %constant.23.clone.refs_5_) | copy-start | bytes 786436

commit v4 on v3

--- a/solution.py
+++ b/solution.py
@@ -235,16 +235,15 @@
         jumps[target] = jumps[target] + scale * rows[at : at + 1]
 
 
-def by_field_order(jumps, values):
+def by_field_order(jumps, values, dim):
     low = low_half(128)
-    for dim in range(3):
-        at = slice(128 * dim, 128 * dim + 128)
-        for pair in range(3):
-            lanes = slice(128 * pair, 128 * pair + 128)
-            front = jumps[256 * dim : 256 * dim + 128, lanes]
-            back = jumps[256 * dim + 128 : 256 * dim + 256, lanes]
-            values[rows_of(2 * pair), at] = jnp.where(low, front, swap_halves(back))
-            values[rows_of(2 * pair + 1), at] = jnp.where(low, swap_halves(front), back)
+    at = slice(128 * dim, 128 * dim + 128)
+    for pair in range(3):
+        lanes = slice(128 * pair, 128 * pair + 128)
+        front = jumps[256 * dim : 256 * dim + 128, lanes]
+        back = jumps[256 * dim + 128 : 256 * dim + 256, lanes]
+        values[rows_of(2 * pair), at] = jnp.where(low, front, swap_halves(back))
+        values[rows_of(2 * pair + 1), at] = jnp.where(low, swap_halves(front), back)
 
 
 def add_surface(values, flux, penalty, factor, surfaces, lift, out, out_far, ready, done):
@@ -302,6 +301,9 @@
         [flux, penalty, d0, d1, d2, owner, levels_near],
         arrivals.at[9:16],
     )
+    later = start_all(
+        [table_far, large_far, both_far, lift_far], [table, large, both, lift], arrivals.at[17:21]
+    )
     for copy in copies[:3]:
         copy.wait()
     level = column_of(levels[...])
@@ -329,10 +331,7 @@
         high = value.astype(BF16)
         pieces[0, rows] = high
         pieces[1, rows] = (value - high.astype(F32)).astype(BF16)
-    later = start_all(
-        [table_far, large_far, both_far, lift_far], [table, large, both, lift], arrivals.at[17:21]
-    )
-    for copy in copies[6:9]:
+    for copy in later + copies[4:11]:
         copy.wait()
 
     def apply(lanes, deriv):
@@ -344,19 +343,6 @@
         lanes = slice(256 * half, 256 * half + 256)
         grads[1, :, lanes] = apply(lanes, d1)
         grads[2, :, lanes] = apply(lanes, d2)
-    for copy in later + copies[4:6]:
-        copy.wait()
-    for first in range(0, 128, 16):
-        scale = amount[first : first + 16]
-        scale = jnp.concatenate([scale] * 4, 1)
-        for field in range(6):
-            total = None
-            for dim in range(3):
-                for other in range(6):
-                    rows = slice(128 * other + first, 128 * other + first + 16)
-                    term = flux[dim, field, other] * grads[dim, rows, :]
-                    total = term if total is None else total + term
-            out[128 * field + first : 128 * field + first + 16] = scale * total
     for pair in range(3):
         for piece, value in enumerate(split3(table[pair])):
             first = 384 * piece + 128 * pair
@@ -373,12 +359,28 @@
         ],
         1,
     )
-    total = mm(matrix[...], traces[...])
-    jumps[0:768] = total[:, 0:384] + total[:, 384:768] + total[:, 768:1152]
-    copies[9].wait()
-    copies[10].wait()
+    jumps[...] = jnp.zeros((776, 384), F32)
     add_owned(jumps, owner, levels_near, back, 1.0)
-    by_field_order(jumps, values)
+
+    def mix(first):
+        scale = amount[first : first + 16]
+        scale = jnp.concatenate([scale] * 4, 1)
+        for field in range(6):
+            total = None
+            for dim in range(3):
+                for other in range(6):
+                    rows = slice(128 * other + first, 128 * other + first + 16)
+                    term = flux[dim, field, other] * grads[dim, rows, :]
+                    total = term if total is None else total + term
+            out[128 * field + first : 128 * field + first + 16] = scale * total
+
+    for dim in range(3):
+        rows = slice(256 * dim, 256 * dim + 256)
+        total = mm(matrix[rows], traces[...])
+        for first in range(48 * dim, min(48 * dim + 48, 128), 16):
+            mix(first)
+        jumps[rows] += total[:, 0:384] + total[:, 384:768] + total[:, 768:1152]
+        by_field_order(jumps, values, dim)
     leaving = add_surface(
         values, flux, penalty, 0.5 * STEP_SIZE * edge, surfaces, lift, out, out_far,
         lambda pair: None, sent,
@@ -423,12 +425,15 @@
                 extra[128 + 32 * q : 160 + 32 * q, lanes] = value[
                     32 * part : 32 * part + 32, 128 * q : 128 * q + 128
                 ]
-    total = mm(remote[...], extra[...])
-    jumps[0:768] = total[:, 0:384] + total[:, 384:768] + total[:, 768:1152]
     for copy in copies[:5]:
         copy.wait()
+    jumps[...] = jnp.zeros((776, 384), F32)
     add_owned(jumps, owner, levels, jnp.concatenate(got_back, 1), -1.0)
-    by_field_order(jumps, values)
+    for dim in range(3):
+        rows = slice(256 * dim, 256 * dim + 256)
+        total = mm(remote[rows], extra[...])
+        jumps[rows] += total[:, 0:384] + total[:, 384:768] + total[:, 768:1152]
+        by_field_order(jumps, values, dim)
     sent = add_surface(
         values, flux, penalty, 0.5 * STEP_SIZE * edge, surfaces, lift, out, out_far,
         lambda pair: copies[5 + pair].wait(), done,

time: 52.4 us -> 51.3 us (0.979)
  Pallas kernels: 19.4 us -> 18.3 us
    pallas_call x1, Pallas kernels: 11.3 us -> 10.7 us  [per_device(): pl.pallas_call(mid, out_shape=shape((768, 512)), in_specs=[HBM] * 14, out...]
  transfers between devices with their start and end apart: 5 -> 5, of which waited for: 0 -> 0; matrix products, arithmetic and copies ran while one was open for 0% -> 0% of each run, Pallas kernels for 22% -> 21%
where the time goes in v4:
time: 51.3 us; the launch traced here: 51 us
  starting transfers between devices  32.3 us (63%)
  Pallas kernels  18.3 us (36%)
    ppermute x4, starting transfers between devices, shifted(): return lax.ppermute(value, axis, pairs)  22.1 us
    pallas_call x1, Pallas kernels, per_device(): pl.pallas_call(mid, out_shape=shape((768, 512)), in_specs=[HBM] * 14, out...  10.7 us
    all_to_all x1, starting transfers between devices, per_device(): lax.all_to_all(mort.reshape(32, 8, 128), 'gy', split_axis=0, concat_axis=...  10.2 us
    pallas_call x1, Pallas kernels, per_device(): pl.pallas_call(pre_kernel, out_shape=[shape((32, 384))] * 4 + [shape((256...  4.05 us
    pallas_call x1, Pallas kernels, per_device(): pl.pallas_call(post, out_shape=shape((768, 512)), in_specs=[VMEM] * 9 + [...  3.61 us
  transfers between devices with their start and end apart: 5, of which 0 were waited for; matrix products, arithmetic and copies ran while one was open for 0% of the time, Pallas kernels for 21%

profile of v4, /device:TPU:8, one launch (start us, length us, event | category | flops | bytes accessed | tf_op | source)
XLA Modules:
  0.0 51.0 jit_solution(769932012524381529)
XLA Ops:
  0.0 4.0 %pre.1 = (f32[32,384]{1,0:T(8,128)}, f32[32,384]{1,0:T(8,128)}, f32[32,384]{1,0:T(8,128)}, f32[32,384]{1,0:T(8,128)}, f32[256,128]{1,0:T(8,128)}, /*index=5*/f32[3,768,128]{2,1,0:T(8,128)}, f32[32,384]{1,0:T(8,128)}) custom-call(f32[768,512]{1,0:T(8,128)} %bitcast.28, s32[4,32]{1,0:T(4,128)} %bitcast.30, s32[1,32]{1,0:T(1,128)} %bitcast.21, ...), custom_call_target="tpu_custom_call" | custom-call | flops 1000000000 | bytes 4194304 | tf_op jit(solution)/shard_map/pre/pallas_call | solution.py:458
  4.1 10.2 %all-to-all-start = ((f32[32,8,128]{2,1,0:T(8,128)}), f32[32,8,128]{2,1,0:T(8,128)S(1)}, u32[]{:S(2)}, u32[]{:S(2)}) async-start(f32[32,8,128]{2,1,0:T(8,128)} %bitcast.27), calls=%async_computation | async-start | bytes 262144 | tf_op jit(solution)/shard_map/all_to_all | solution.py:485
  14.2 14.1 %collective-permute-start = (f32[32,384]{1,0:T(8,128)}, f32[32,384]{1,0:T(8,128)S(1)}, u32[]{:S(2)}, u32[]{:S(2)}) collective-permute-start(f32[32,384]{1,0:T(8,128)} %get-tuple-element.13), channel_id=1, source_target_pairs={{0,510},{1,511},{2,0},{3,1},{4,2},{5,3},{6,4},{7,5},{8,6},{9,7},{1... | collective-permute-start | bytes 147464 | tf_op jit(solution)/shard_map/ppermute | solution.py:25
  28.4 3.4 %collective-permute-start.1 = (f32[32,384]{1,0:T(8,128)}, f32[32,384]{1,0:T(8,128)S(1)}, u32[]{:S(2)}, u32[]{:S(2)}) collective-permute-start(f32[32,384]{1,0:T(8,128)} %get-tuple-element.14), channel_id=1, source_target_pairs={{0,511},{1,0},{2,1},{3,2},{4,3},{5,4},{6,5},{7,6},{8,7},{9,8},{10,... | collective-permute-start | bytes 147464 | tf_op jit(solution)/shard_map/ppermute | solution.py:25
  31.8 2.5 %collective-permute-start.2 = (f32[32,384]{1,0:T(8,128)}, f32[32,384]{1,0:T(8,128)S(1)}, u32[]{:S(2)}, u32[]{:S(2)}) collective-permute-start(f32[32,384]{1,0:T(8,128)} %get-tuple-element.15), channel_id=1, source_target_pairs={{0,1},{1,2},{2,3},{3,4},{4,5},{5,6},{6,7},{7,8},{8,9},{9,10},{10,1... | collective-permute-start | bytes 147464 | tf_op jit(solution)/shard_map/ppermute | solution.py:25
  34.2 2.1 %collective-permute-start.3 = (f32[32,384]{1,0:T(8,128)}, f32[32,384]{1,0:T(8,128)S(1)}, u32[]{:S(2)}, u32[]{:S(2)}) collective-permute-start(f32[32,384]{1,0:T(8,128)} %get-tuple-element.16), channel_id=1, source_target_pairs={{0,2},{1,3},{2,4},{3,5},{4,6},{5,7},{6,8},{7,9},{8,10},{9,11},{10,... | collective-permute-start | bytes 147464 | tf_op jit(solution)/shard_map/ppermute | solution.py:25
  36.3 0.0 copy-start
  36.4 0.0 copy-start.1
  36.4 0.0 copy-start.2
  36.4 0.0 copy-start.3
  36.4 0.0 copy-start.4
  36.4 0.0 copy-start.5
  36.4 0.0 copy-start.6
  36.4 0.0 copy-start.7
  36.4 10.7 %mid.1.refs_14_ = f32[768,512]{1,0:T(8,128)} custom-call(s32[1,128]{1,0:T(1,128)} %bitcast.24, s32[4,32]{1,0:T(4,128)} %bitcast.19, s32[6,128]{1,0:T(8,128)} %bitcast.16, f32[3,6,6]{2,1,0:T(8,128)} %refs_9_.2, f32[6]{0:T(128)} %refs_10_.1, s32[1,32]{1,0:T(1,128)} %bitcast.22, f32[768,512]{1,0:T(8,128)} %bitcast.29, ...), custom_call_target="tpu_custom_call" | custom-call | flops 8000000000 | bytes 8388608 | tf_op jit(solution)/shard_map/mid/pallas_call | solution.py:491
  47.1 0.0 collective-permute-done.refs_1_
  47.2 0.0 collective-permute-done.1.refs_2_
  47.2 0.0 collective-permute-done.2.refs_3_
  47.2 0.0 collective-permute-done.3.refs_4_
  47.2 0.0 all-to-all-done
  47.2 0.0 copy-done
  47.2 0.0 copy-done.1
  47.2 0.0 copy-done.2
  47.3 3.6 %post.1 = f32[768,512]{1,0:T(8,128)} custom-call(f32[256,128]{1,0:T(8,128)S(1)} %bitcast.15, f32[32,384]{1,0:T(8,128)S(1)} %collective-permute-done.refs_1_, f32[32,384]{1,0:T(8,128)S(1)} %collective-permute-done.1.refs_2_, f32[32,384]{1,0:T(8,128)S(1)} %collective-permute-done.2.refs_3_, ...), custom_call_target="tpu_custom_call", output_to_operand_aliasing={{}: (14, {})} | custom-call | flops 2000000000 | bytes 4194304 | tf_op jit(solution)/shard_map/post/pallas_call | solution.py:547
  (5 shorter events, 0.0 us)
Async XLA Ops:
  4.1 43.1 %all-to-all-start = ((f32[32,8,128]{2,1,0:T(8,128)}), f32[32,8,128]{2,1,0:T(8,128)S(1)}, u32[]{:S(2)}, u32[]{:S(2)}) async-start(f32[32,8,128]{2,1,0:T(8,128)} %bitcast.27), calls=%async_computation | async-start | bytes 262144 | tf_op jit(solution)/shard_map/all_to_all | solution.py:485
  14.2 32.9 %collective-permute-start = (f32[32,384]{1,0:T(8,128)}, f32[32,384]{1,0:T(8,128)S(1)}, u32[]{:S(2)}, u32[]{:S(2)}) collective-permute-start(f32[32,384]{1,0:T(8,128)} %get-tuple-element.13), channel_id=1, source_target_pairs={{0,510},{1,511},{2,0},{3,1},{4,2},{5,3},{6,4},{7,5},{8,6},{9,7},{1... | collective-permute-start | bytes 147464 | tf_op jit(solution)/shard_map/ppermute | solution.py:25
  28.4 18.8 %collective-permute-start.1 = (f32[32,384]{1,0:T(8,128)}, f32[32,384]{1,0:T(8,128)S(1)}, u32[]{:S(2)}, u32[]{:S(2)}) collective-permute-start(f32[32,384]{1,0:T(8,128)} %get-tuple-element.14), channel_id=1, source_target_pairs={{0,511},{1,0},{2,1},{3,2},{4,3},{5,4},{6,5},{7,6},{8,7},{9,8},{10,... | collective-permute-start | bytes 147464 | tf_op jit(solution)/shard_map/ppermute | solution.py:25
  31.8 15.4 %collective-permute-start.2 = (f32[32,384]{1,0:T(8,128)}, f32[32,384]{1,0:T(8,128)S(1)}, u32[]{:S(2)}, u32[]{:S(2)}) collective-permute-start(f32[32,384]{1,0:T(8,128)} %get-tuple-element.15), channel_id=1, source_target_pairs={{0,1},{1,2},{2,3},{3,4},{4,5},{5,6},{6,7},{7,8},{8,9},{9,10},{10,1... | collective-permute-start | bytes 147464 | tf_op jit(solution)/shard_map/ppermute | solution.py:25
  34.2 12.9 %collective-permute-start.3 = (f32[32,384]{1,0:T(8,128)}, f32[32,384]{1,0:T(8,128)S(1)}, u32[]{:S(2)}, u32[]{:S(2)}) collective-permute-start(f32[32,384]{1,0:T(8,128)} %get-tuple-element.16), channel_id=1, source_target_pairs={{0,2},{1,3},{2,4},{3,5},{4,6},{5,7},{6,8},{7,9},{8,10},{9,11},{10,... | collective-permute-start | bytes 147464 | tf_op jit(solution)/shard_map/ppermute | solution.py:25
  36.3 10.8 %copy-start = (f32[3,6,6]{2,1,0:T(8,128)S(1)}, f32[3,6,6]{2,1,0:T(8,128)}, u32[]{:S(2)}) copy-start(f32[3,6,6]{2,1,0:T(8,128)} %refs_9_.2) | copy-start | bytes 1300
  36.4 10.8 %copy-start.1 = (s32[768]{0:T(1024)S(1)}, s32[768]{0:T(1024)}, u32[]{:S(2)}) copy-start(s32[768]{0:T(1024)} %param.18) | copy-start | bytes 9220
  36.4 10.8 %copy-start.2 = (s32[1,32,4]{1,2,0:T(4,128)S(1)}, s32[1,32,4]{1,2,0:T(4,128)}, u32[]{:S(2)}) copy-start(s32[1,32,4]{1,2,0:T(4,128)} %param.21) | copy-start | bytes 1540
  36.4 10.8 %copy-start.3 = (s32[1,32,1]{1,2,0:T(1,128)S(1)}, s32[1,32,1]{1,2,0:T(1,128)}, u32[]{:S(2)}) copy-start(s32[1,32,1]{1,2,0:T(1,128)} %param.20) | copy-start | bytes 388
  36.4 10.8 %copy-start.4 = (s32[128]{0:T(128)S(1)}, s32[128]{0:T(128)}, u32[]{:S(2)}) copy-start(s32[128]{0:T(128)} %param.17) | copy-start | bytes 1540
  36.4 10.8 %copy-start.5 = (f32[6]{0:T(128)S(1)}, f32[6]{0:T(128)}, u32[]{:S(2)}) copy-start(f32[6]{0:T(128)} %refs_10_.1) | copy-start | bytes 76
  36.4 10.8 %copy-start.6 = (bf16[512,512]{1,0:T(8,128)(2,1)S(1)}, bf16[512,512]{1,0:T(8,128)(2,1)}, u32[]{:S(2)}) copy-start(bf16[512,512]{1,0:T(8,128)(2,1)} %constant.22.clone.refs_13_) | copy-start | bytes 1572868
  36.4 10.8 %copy-start.7 = (f32[128,512]{1,0:T(8,128)S(1)}, f32[128,512]{1,0:T(8,128)}, u32[]{:S(2)}) copy-start(f32[128,512]{1,0:T(8,128)} %constant.23.clone.refs_5_) | copy-start | bytes 786436

commit v5 on v4

--- a/solution.py
+++ b/solution.py
@@ -161,6 +161,7 @@
     inner = (
         mm(pieces[0], select[...]) + mm(pieces[1], select[...]) + mm(pieces[2], select[...])
     )
+    leaving = []
     for pair in range(3):
         even, odd = rows_of(2 * pair), rows_of(2 * pair + 1)
         fronts = [(state[even, :128], state[odd, :128])]
@@ -174,7 +175,7 @@
             back = jnp.where(low, swap_halves(backs[dim][0]), backs[dim][1])
             table[pair, pl.ds(2 * dim, 128, stride=6), :] = front
             table[pair, pl.ds(2 * dim + 1, 128, stride=6), :] = back
-    leaving = start_all([table.at[:, 0:768]], [table_far], sent)
+        leaving += start_all([table.at[pair, 0:768]], [table_far.at[pair]], sent.at[7 + pair : 8 + pair])
     for copy in copies[7:]:
         copy.wait()
 
@@ -331,18 +332,9 @@
         high = value.astype(BF16)
         pieces[0, rows] = high
         pieces[1, rows] = (value - high.astype(F32)).astype(BF16)
-    for copy in later + copies[4:11]:
+    for copy in copies[4:11] + later:
         copy.wait()
 
-    def apply(lanes, deriv):
-        high, rest = pieces[0, :, lanes], pieces[1, :, lanes]
-        return mm(high, deriv[0]) + (mm(high, deriv[1]) + mm(rest, deriv[0]))
-
-    grads[0] = apply(slice(0, 512), d0)
-    for half in range(2):
-        lanes = slice(256 * half, 256 * half + 256)
-        grads[1, :, lanes] = apply(lanes, d1)
-        grads[2, :, lanes] = apply(lanes, d2)
     for pair in range(3):
         for piece, value in enumerate(split3(table[pair])):
             first = 384 * piece + 128 * pair
@@ -362,6 +354,15 @@
     jumps[...] = jnp.zeros((776, 384), F32)
     add_owned(jumps, owner, levels_near, back, 1.0)
 
+    def apply(lanes, deriv):
+        high, rest = pieces[0, :, lanes], pieces[1, :, lanes]
+        return mm(high, deriv[0]) + (mm(high, deriv[1]) + mm(rest, deriv[0]))
+
+    grads[0] = apply(slice(0, 512), d0)
+    for half in range(2):
+        lanes = slice(256 * half, 256 * half + 256)
+        grads[1, :, lanes] = apply(lanes, d1)
+        grads[2, :, lanes] = apply(lanes, d2)
     def mix(first):
         scale = amount[first : first + 16]
         scale = jnp.concatenate([scale] * 4, 1)
@@ -473,7 +474,7 @@
             pltpu.VMEM((288, 384), F32),
             pltpu.VMEM((256, 128), F32),
             pltpu.SemaphoreType.DMA((11,)),
-            pltpu.SemaphoreType.DMA((7,)),
+            pltpu.SemaphoreType.DMA((10,)),
         ],
         compiler_params=params(60),
         cost_estimate=pl.CostEstimate(flops=10**9, bytes_accessed=4 << 20, transcendentals=0),

time: 51.3 us -> 51.1 us (level)
  no operation moved by 1% of the time
where the time goes in v5:
time: 51.1 us; the launch traced here: 50.8 us
  starting transfers between devices  32.3 us (63%)
  Pallas kernels  18.1 us (35%)
    ppermute x4, starting transfers between devices, shifted(): return lax.ppermute(value, axis, pairs)  22.1 us
    pallas_call x1, Pallas kernels, per_device(): pl.pallas_call(mid, out_shape=shape((768, 512)), in_specs=[HBM] * 14, out...  10.4 us
    all_to_all x1, starting transfers between devices, per_device(): lax.all_to_all(mort.reshape(32, 8, 128), 'gy', split_axis=0, concat_axis=...  10.2 us
    pallas_call x1, Pallas kernels, per_device(): pl.pallas_call(pre_kernel, out_shape=[shape((32, 384))] * 4 + [shape((256...  4.09 us
    pallas_call x1, Pallas kernels, per_device(): pl.pallas_call(post, out_shape=shape((768, 512)), in_specs=[VMEM] * 9 + [...  3.6 us
  transfers between devices with their start and end apart: 5, of which 0 were waited for; matrix products, arithmetic and copies ran while one was open for 0% of the time, Pallas kernels for 21%

profile of v5, /device:TPU:8, one launch (start us, length us, event | category | flops | bytes accessed | tf_op | source)
XLA Modules:
  0.0 50.8 jit_solution(10020873555069696935)
XLA Ops:
  0.0 4.1 %pre.1 = (f32[32,384]{1,0:T(8,128)}, f32[32,384]{1,0:T(8,128)}, f32[32,384]{1,0:T(8,128)}, f32[32,384]{1,0:T(8,128)}, f32[256,128]{1,0:T(8,128)}, /*index=5*/f32[3,768,128]{2,1,0:T(8,128)}, f32[32,384]{1,0:T(8,128)}) custom-call(f32[768,512]{1,0:T(8,128)} %bitcast.28, s32[4,32]{1,0:T(4,128)} %bitcast.30, s32[1,32]{1,0:T(1,128)} %bitcast.21, ...), custom_call_target="tpu_custom_call" | custom-call | flops 1000000000 | bytes 4194304 | tf_op jit(solution)/shard_map/pre/pallas_call | solution.py:459
  4.1 10.2 %all-to-all-start = ((f32[32,8,128]{2,1,0:T(8,128)}), f32[32,8,128]{2,1,0:T(8,128)S(1)}, u32[]{:S(2)}, u32[]{:S(2)}) async-start(f32[32,8,128]{2,1,0:T(8,128)} %bitcast.27), calls=%async_computation | async-start | bytes 262144 | tf_op jit(solution)/shard_map/all_to_all | solution.py:486
  14.3 14.1 %collective-permute-start = (f32[32,384]{1,0:T(8,128)}, f32[32,384]{1,0:T(8,128)S(1)}, u32[]{:S(2)}, u32[]{:S(2)}) collective-permute-start(f32[32,384]{1,0:T(8,128)} %get-tuple-element.13), channel_id=1, source_target_pairs={{0,510},{1,511},{2,0},{3,1},{4,2},{5,3},{6,4},{7,5},{8,6},{9,7},{1... | collective-permute-start | bytes 147464 | tf_op jit(solution)/shard_map/ppermute | solution.py:25
  28.4 3.4 %collective-permute-start.1 = (f32[32,384]{1,0:T(8,128)}, f32[32,384]{1,0:T(8,128)S(1)}, u32[]{:S(2)}, u32[]{:S(2)}) collective-permute-start(f32[32,384]{1,0:T(8,128)} %get-tuple-element.14), channel_id=1, source_target_pairs={{0,511},{1,0},{2,1},{3,2},{4,3},{5,4},{6,5},{7,6},{8,7},{9,8},{10,... | collective-permute-start | bytes 147464 | tf_op jit(solution)/shard_map/ppermute | solution.py:25
  31.8 2.5 %collective-permute-start.2 = (f32[32,384]{1,0:T(8,128)}, f32[32,384]{1,0:T(8,128)S(1)}, u32[]{:S(2)}, u32[]{:S(2)}) collective-permute-start(f32[32,384]{1,0:T(8,128)} %get-tuple-element.15), channel_id=1, source_target_pairs={{0,1},{1,2},{2,3},{3,4},{4,5},{5,6},{6,7},{7,8},{8,9},{9,10},{10,1... | collective-permute-start | bytes 147464 | tf_op jit(solution)/shard_map/ppermute | solution.py:25
  34.3 2.1 %collective-permute-start.3 = (f32[32,384]{1,0:T(8,128)}, f32[32,384]{1,0:T(8,128)S(1)}, u32[]{:S(2)}, u32[]{:S(2)}) collective-permute-start(f32[32,384]{1,0:T(8,128)} %get-tuple-element.16), channel_id=1, source_target_pairs={{0,2},{1,3},{2,4},{3,5},{4,6},{5,7},{6,8},{7,9},{8,10},{9,11},{10,... | collective-permute-start | bytes 147464 | tf_op jit(solution)/shard_map/ppermute | solution.py:25
  36.4 0.0 copy-start
  36.4 0.0 copy-start.1
  36.4 0.0 copy-start.2
  36.4 0.0 copy-start.3
  36.4 0.0 copy-start.4
  36.5 0.0 copy-start.5
  36.5 0.0 copy-start.6
  36.5 0.0 copy-start.7
  36.5 10.4 %mid.1.refs_14_ = f32[768,512]{1,0:T(8,128)} custom-call(s32[1,128]{1,0:T(1,128)} %bitcast.24, s32[4,32]{1,0:T(4,128)} %bitcast.19, s32[6,128]{1,0:T(8,128)} %bitcast.16, f32[3,6,6]{2,1,0:T(8,128)} %refs_9_.2, f32[6]{0:T(128)} %refs_10_.1, s32[1,32]{1,0:T(1,128)} %bitcast.22, f32[768,512]{1,0:T(8,128)} %bitcast.29, ...), custom_call_target="tpu_custom_call" | custom-call | flops 8000000000 | bytes 8388608 | tf_op jit(solution)/shard_map/mid/pallas_call | solution.py:492
  46.9 0.0 collective-permute-done.refs_1_
  46.9 0.0 collective-permute-done.1.refs_2_
  47.0 0.0 collective-permute-done.2.refs_3_
  47.0 0.0 collective-permute-done.3.refs_4_
  47.0 0.0 all-to-all-done
  47.0 0.0 copy-done
  47.0 0.0 copy-done.1
  47.0 0.0 copy-done.2
  47.1 3.6 %post.1 = f32[768,512]{1,0:T(8,128)} custom-call(f32[256,128]{1,0:T(8,128)S(1)} %bitcast.15, f32[32,384]{1,0:T(8,128)S(1)} %collective-permute-done.refs_1_, f32[32,384]{1,0:T(8,128)S(1)} %collective-permute-done.1.refs_2_, f32[32,384]{1,0:T(8,128)S(1)} %collective-permute-done.2.refs_3_, ...), custom_call_target="tpu_custom_call", output_to_operand_aliasing={{}: (14, {})} | custom-call | flops 2000000000 | bytes 4194304 | tf_op jit(solution)/shard_map/post/pallas_call | solution.py:548
  (5 shorter events, 0.0 us)
Async XLA Ops:
  4.1 42.9 %all-to-all-start = ((f32[32,8,128]{2,1,0:T(8,128)}), f32[32,8,128]{2,1,0:T(8,128)S(1)}, u32[]{:S(2)}, u32[]{:S(2)}) async-start(f32[32,8,128]{2,1,0:T(8,128)} %bitcast.27), calls=%async_computation | async-start | bytes 262144 | tf_op jit(solution)/shard_map/all_to_all | solution.py:486
  14.3 32.7 %collective-permute-start = (f32[32,384]{1,0:T(8,128)}, f32[32,384]{1,0:T(8,128)S(1)}, u32[]{:S(2)}, u32[]{:S(2)}) collective-permute-start(f32[32,384]{1,0:T(8,128)} %get-tuple-element.13), channel_id=1, source_target_pairs={{0,510},{1,511},{2,0},{3,1},{4,2},{5,3},{6,4},{7,5},{8,6},{9,7},{1... | collective-permute-start | bytes 147464 | tf_op jit(solution)/shard_map/ppermute | solution.py:25
  28.4 18.5 %collective-permute-start.1 = (f32[32,384]{1,0:T(8,128)}, f32[32,384]{1,0:T(8,128)S(1)}, u32[]{:S(2)}, u32[]{:S(2)}) collective-permute-start(f32[32,384]{1,0:T(8,128)} %get-tuple-element.14), channel_id=1, source_target_pairs={{0,511},{1,0},{2,1},{3,2},{4,3},{5,4},{6,5},{7,6},{8,7},{9,8},{10,... | collective-permute-start | bytes 147464 | tf_op jit(solution)/shard_map/ppermute | solution.py:25
  31.8 15.2 %collective-permute-start.2 = (f32[32,384]{1,0:T(8,128)}, f32[32,384]{1,0:T(8,128)S(1)}, u32[]{:S(2)}, u32[]{:S(2)}) collective-permute-start(f32[32,384]{1,0:T(8,128)} %get-tuple-element.15), channel_id=1, source_target_pairs={{0,1},{1,2},{2,3},{3,4},{4,5},{5,6},{6,7},{7,8},{8,9},{9,10},{10,1... | collective-permute-start | bytes 147464 | tf_op jit(solution)/shard_map/ppermute | solution.py:25
  34.3 12.7 %collective-permute-start.3 = (f32[32,384]{1,0:T(8,128)}, f32[32,384]{1,0:T(8,128)S(1)}, u32[]{:S(2)}, u32[]{:S(2)}) collective-permute-start(f32[32,384]{1,0:T(8,128)} %get-tuple-element.16), channel_id=1, source_target_pairs={{0,2},{1,3},{2,4},{3,5},{4,6},{5,7},{6,8},{7,9},{8,10},{9,11},{10,... | collective-permute-start | bytes 147464 | tf_op jit(solution)/shard_map/ppermute | solution.py:25
  36.4 10.6 %copy-start = (f32[3,6,6]{2,1,0:T(8,128)S(1)}, f32[3,6,6]{2,1,0:T(8,128)}, u32[]{:S(2)}) copy-start(f32[3,6,6]{2,1,0:T(8,128)} %refs_9_.2) | copy-start | bytes 1300
  36.4 10.6 %copy-start.1 = (s32[768]{0:T(1024)S(1)}, s32[768]{0:T(1024)}, u32[]{:S(2)}) copy-start(s32[768]{0:T(1024)} %param.18) | copy-start | bytes 9220
  36.4 10.6 %copy-start.2 = (s32[1,32,4]{1,2,0:T(4,128)S(1)}, s32[1,32,4]{1,2,0:T(4,128)}, u32[]{:S(2)}) copy-start(s32[1,32,4]{1,2,0:T(4,128)} %param.21) | copy-start | bytes 1540
  36.4 10.6 %copy-start.3 = (s32[1,32,1]{1,2,0:T(1,128)S(1)}, s32[1,32,1]{1,2,0:T(1,128)}, u32[]{:S(2)}) copy-start(s32[1,32,1]{1,2,0:T(1,128)} %param.20) | copy-start | bytes 388
  36.4 10.6 %copy-start.4 = (s32[128]{0:T(128)S(1)}, s32[128]{0:T(128)}, u32[]{:S(2)}) copy-start(s32[128]{0:T(128)} %param.17) | copy-start | bytes 1540
  36.5 10.6 %copy-start.5 = (f32[6]{0:T(128)S(1)}, f32[6]{0:T(128)}, u32[]{:S(2)}) copy-start(f32[6]{0:T(128)} %refs_10_.1) | copy-start | bytes 76
  36.5 10.6 %copy-start.6 = (bf16[512,512]{1,0:T(8,128)(2,1)S(1)}, bf16[512,512]{1,0:T(8,128)(2,1)}, u32[]{:S(2)}) copy-start(bf16[512,512]{1,0:T(8,128)(2,1)} %constant.22.clone.refs_13_) | copy-start | bytes 1572868
  36.5 10.6 %copy-start.7 = (f32[128,512]{1,0:T(8,128)S(1)}, f32[128,512]{1,0:T(8,128)}, u32[]{:S(2)}) copy-start(f32[128,512]{1,0:T(8,128)} %constant.23.clone.refs_5_) | copy-start | bytes 786436

commit v6 on v5

--- a/solution.py
+++ b/solution.py
@@ -378,7 +378,7 @@
     for dim in range(3):
         rows = slice(256 * dim, 256 * dim + 256)
         total = mm(matrix[rows], traces[...])
-        for first in range(48 * dim, min(48 * dim + 48, 128), 16):
+        for first in ((0, 16), (32, 48, 64), (80, 96, 112))[dim]:
             mix(first)
         jumps[rows] += total[:, 0:384] + total[:, 384:768] + total[:, 768:1152]
         by_field_order(jumps, values, dim)
@@ -402,6 +402,21 @@
         [flux, penalty, owner, levels, lift, *(out.at[rows] for rows in thirds)],
         arrivals,
     )
+    for place, rows in enumerate((a0, a1, a2, a3)):
+        for piece, value in enumerate(split3(rows[...])):
+            extra[32 * place : 32 * place + 32, 384 * piece : 384 * piece + 384] = value
+    got_back = [got[pl.ds(part, 32, stride=8), :] for part in range(3)]
+    got_large = [got[pl.ds(3 + part, 32, stride=8), :] for part in range(3)]
+    onto = jnp.dot(
+        jnp.concatenate(got_large, 0), project[...], precision=HIGHEST, preferred_element_type=F32
+    )
+    for piece, value in enumerate(split3(onto)):
+        for part in range(3):
+            lanes = slice(384 * piece + 128 * part, 384 * piece + 128 * part + 128)
+            for q in range(4):
+                extra[128 + 32 * q : 160 + 32 * q, lanes] = value[
+                    32 * part : 32 * part + 32, 128 * q : 128 * q + 128
+                ]
     minus = -(1 << column_of(levels_row[...])).astype(F32)
     element = lax.broadcasted_iota(jnp.int32, (128, 1), 0)
     arrived_slot = 768 + lax.broadcasted_iota(jnp.int32, (1, 128), 1)
@@ -411,21 +426,6 @@
         wanted, mine = wanted_column(sources, face), 6 * element + face
         remote[rows_of(face), 0:128] = jnp.where(wanted == arrived_slot, minus, 0.0).astype(BF16)
         remote[rows_of(face), 128:256] = jnp.where(mine == child_row, minus, 0.0).astype(BF16)
-    for place, rows in enumerate((a0, a1, a2, a3)):
-        for piece, value in enumerate(split3(rows[...])):
-            extra[32 * place : 32 * place + 32, 384 * piece : 384 * piece + 384] = value
-    got_back = [got[pl.ds(part, 32, stride=8), :] for part in range(3)]
-    got_large = [got[pl.ds(3 + part, 32, stride=8), :] for part in range(3)]
-    onto = jnp.dot(
-        jnp.concatenate(got_large, 0), project[...], precision=HIGHEST, preferred_element_type=F32
-    )
-    for piece, value in enumerate(split3(onto)):
-        for part in range(3):
-            lanes = slice(384 * piece + 128 * part, 384 * piece + 128 * part + 128)
-            for q in range(4):
-                extra[128 + 32 * q : 160 + 32 * q, lanes] = value[
-                    32 * part : 32 * part + 32, 128 * q : 128 * q + 128
-                ]
     for copy in copies[:5]:
         copy.wait()
     jumps[...] = jnp.zeros((776, 384), F32)

time: 51.1 us -> 51.1 us (level)
  no operation moved by 1% of the time
where the time goes in v6:
time: 51.1 us; the launch traced here: 50.9 us
  starting transfers between devices  32.3 us (63%)
  Pallas kernels  18.2 us (36%)
    ppermute x4, starting transfers between devices, shifted(): return lax.ppermute(value, axis, pairs)  22.1 us
    pallas_call x1, Pallas kernels, per_device(): pl.pallas_call(mid, out_shape=shape((768, 512)), in_specs=[HBM] * 14, out...  10.5 us
    all_to_all x1, starting transfers between devices, per_device(): lax.all_to_all(mort.reshape(32, 8, 128), 'gy', split_axis=0, concat_axis=...  10.2 us
    pallas_call x1, Pallas kernels, per_device(): pl.pallas_call(pre_kernel, out_shape=[shape((32, 384))] * 4 + [shape((256...  4.09 us
    pallas_call x1, Pallas kernels, per_device(): pl.pallas_call(post, out_shape=shape((768, 512)), in_specs=[VMEM] * 9 + [...  3.61 us
  transfers between devices with their start and end apart: 5, of which 0 were waited for; matrix products, arithmetic and copies ran while one was open for 0% of the time, Pallas kernels for 21%

profile of v6, /device:TPU:8, one launch (start us, length us, event | category | flops | bytes accessed | tf_op | source)
XLA Modules:
  0.0 50.9 jit_solution(12684558495660166286)
XLA Ops:
  0.0 4.1 %pre.1 = (f32[32,384]{1,0:T(8,128)}, f32[32,384]{1,0:T(8,128)}, f32[32,384]{1,0:T(8,128)}, f32[32,384]{1,0:T(8,128)}, f32[256,128]{1,0:T(8,128)}, /*index=5*/f32[3,768,128]{2,1,0:T(8,128)}, f32[32,384]{1,0:T(8,128)}) custom-call(f32[768,512]{1,0:T(8,128)} %bitcast.28, s32[4,32]{1,0:T(4,128)} %bitcast.30, s32[1,32]{1,0:T(1,128)} %bitcast.21, ...), custom_call_target="tpu_custom_call" | custom-call | flops 1000000000 | bytes 4194304 | tf_op jit(solution)/shard_map/pre/pallas_call | solution.py:459
  4.1 10.2 %all-to-all-start = ((f32[32,8,128]{2,1,0:T(8,128)}), f32[32,8,128]{2,1,0:T(8,128)S(1)}, u32[]{:S(2)}, u32[]{:S(2)}) async-start(f32[32,8,128]{2,1,0:T(8,128)} %bitcast.27), calls=%async_computation | async-start | bytes 262144 | tf_op jit(solution)/shard_map/all_to_all | solution.py:486
  14.3 14.1 %collective-permute-start = (f32[32,384]{1,0:T(8,128)}, f32[32,384]{1,0:T(8,128)S(1)}, u32[]{:S(2)}, u32[]{:S(2)}) collective-permute-start(f32[32,384]{1,0:T(8,128)} %get-tuple-element.13), channel_id=1, source_target_pairs={{0,510},{1,511},{2,0},{3,1},{4,2},{5,3},{6,4},{7,5},{8,6},{9,7},{1... | collective-permute-start | bytes 147464 | tf_op jit(solution)/shard_map/ppermute | solution.py:25
  28.4 3.4 %collective-permute-start.1 = (f32[32,384]{1,0:T(8,128)}, f32[32,384]{1,0:T(8,128)S(1)}, u32[]{:S(2)}, u32[]{:S(2)}) collective-permute-start(f32[32,384]{1,0:T(8,128)} %get-tuple-element.14), channel_id=1, source_target_pairs={{0,511},{1,0},{2,1},{3,2},{4,3},{5,4},{6,5},{7,6},{8,7},{9,8},{10,... | collective-permute-start | bytes 147464 | tf_op jit(solution)/shard_map/ppermute | solution.py:25
  31.8 2.5 %collective-permute-start.2 = (f32[32,384]{1,0:T(8,128)}, f32[32,384]{1,0:T(8,128)S(1)}, u32[]{:S(2)}, u32[]{:S(2)}) collective-permute-start(f32[32,384]{1,0:T(8,128)} %get-tuple-element.15), channel_id=1, source_target_pairs={{0,1},{1,2},{2,3},{3,4},{4,5},{5,6},{6,7},{7,8},{8,9},{9,10},{10,1... | collective-permute-start | bytes 147464 | tf_op jit(solution)/shard_map/ppermute | solution.py:25
  34.3 2.1 %collective-permute-start.3 = (f32[32,384]{1,0:T(8,128)}, f32[32,384]{1,0:T(8,128)S(1)}, u32[]{:S(2)}, u32[]{:S(2)}) collective-permute-start(f32[32,384]{1,0:T(8,128)} %get-tuple-element.16), channel_id=1, source_target_pairs={{0,2},{1,3},{2,4},{3,5},{4,6},{5,7},{6,8},{7,9},{8,10},{9,11},{10,... | collective-permute-start | bytes 147464 | tf_op jit(solution)/shard_map/ppermute | solution.py:25
  36.4 0.0 copy-start
  36.4 0.0 copy-start.1
  36.4 0.0 copy-start.2
  36.4 0.0 copy-start.3
  36.4 0.0 copy-start.4
  36.5 0.0 copy-start.5
  36.5 0.0 copy-start.6
  36.5 0.0 copy-start.7
  36.5 10.5 %mid.1.refs_14_ = f32[768,512]{1,0:T(8,128)} custom-call(s32[1,128]{1,0:T(1,128)} %bitcast.24, s32[4,32]{1,0:T(4,128)} %bitcast.19, s32[6,128]{1,0:T(8,128)} %bitcast.16, f32[3,6,6]{2,1,0:T(8,128)} %refs_9_.2, f32[6]{0:T(128)} %refs_10_.1, s32[1,32]{1,0:T(1,128)} %bitcast.22, f32[768,512]{1,0:T(8,128)} %bitcast.29, ...), custom_call_target="tpu_custom_call" | custom-call | flops 8000000000 | bytes 8388608 | tf_op jit(solution)/shard_map/mid/pallas_call | solution.py:492
  47.0 0.0 collective-permute-done.refs_1_
  47.0 0.0 collective-permute-done.1.refs_2_
  47.0 0.0 collective-permute-done.2.refs_3_
  47.0 0.0 collective-permute-done.3.refs_4_
  47.0 0.0 all-to-all-done
  47.0 0.0 copy-done
  47.0 0.0 copy-done.1
  47.0 0.0 copy-done.2
  47.1 3.6 %post.1 = f32[768,512]{1,0:T(8,128)} custom-call(f32[256,128]{1,0:T(8,128)S(1)} %bitcast.15, f32[32,384]{1,0:T(8,128)S(1)} %collective-permute-done.refs_1_, f32[32,384]{1,0:T(8,128)S(1)} %collective-permute-done.1.refs_2_, f32[32,384]{1,0:T(8,128)S(1)} %collective-permute-done.2.refs_3_, ...), custom_call_target="tpu_custom_call", output_to_operand_aliasing={{}: (14, {})} | custom-call | flops 2000000000 | bytes 4194304 | tf_op jit(solution)/shard_map/post/pallas_call | solution.py:548
  (5 shorter events, 0.0 us)
Async XLA Ops:
  4.1 42.9 %all-to-all-start = ((f32[32,8,128]{2,1,0:T(8,128)}), f32[32,8,128]{2,1,0:T(8,128)S(1)}, u32[]{:S(2)}, u32[]{:S(2)}) async-start(f32[32,8,128]{2,1,0:T(8,128)} %bitcast.27), calls=%async_computation | async-start | bytes 262144 | tf_op jit(solution)/shard_map/all_to_all | solution.py:486
  14.3 32.7 %collective-permute-start = (f32[32,384]{1,0:T(8,128)}, f32[32,384]{1,0:T(8,128)S(1)}, u32[]{:S(2)}, u32[]{:S(2)}) collective-permute-start(f32[32,384]{1,0:T(8,128)} %get-tuple-element.13), channel_id=1, source_target_pairs={{0,510},{1,511},{2,0},{3,1},{4,2},{5,3},{6,4},{7,5},{8,6},{9,7},{1... | collective-permute-start | bytes 147464 | tf_op jit(solution)/shard_map/ppermute | solution.py:25
  28.4 18.6 %collective-permute-start.1 = (f32[32,384]{1,0:T(8,128)}, f32[32,384]{1,0:T(8,128)S(1)}, u32[]{:S(2)}, u32[]{:S(2)}) collective-permute-start(f32[32,384]{1,0:T(8,128)} %get-tuple-element.14), channel_id=1, source_target_pairs={{0,511},{1,0},{2,1},{3,2},{4,3},{5,4},{6,5},{7,6},{8,7},{9,8},{10,... | collective-permute-start | bytes 147464 | tf_op jit(solution)/shard_map/ppermute | solution.py:25
  31.8 15.2 %collective-permute-start.2 = (f32[32,384]{1,0:T(8,128)}, f32[32,384]{1,0:T(8,128)S(1)}, u32[]{:S(2)}, u32[]{:S(2)}) collective-permute-start(f32[32,384]{1,0:T(8,128)} %get-tuple-element.15), channel_id=1, source_target_pairs={{0,1},{1,2},{2,3},{3,4},{4,5},{5,6},{6,7},{7,8},{8,9},{9,10},{10,1... | collective-permute-start | bytes 147464 | tf_op jit(solution)/shard_map/ppermute | solution.py:25
  34.3 12.7 %collective-permute-start.3 = (f32[32,384]{1,0:T(8,128)}, f32[32,384]{1,0:T(8,128)S(1)}, u32[]{:S(2)}, u32[]{:S(2)}) collective-permute-start(f32[32,384]{1,0:T(8,128)} %get-tuple-element.16), channel_id=1, source_target_pairs={{0,2},{1,3},{2,4},{3,5},{4,6},{5,7},{6,8},{7,9},{8,10},{9,11},{10,... | collective-permute-start | bytes 147464 | tf_op jit(solution)/shard_map/ppermute | solution.py:25
  36.4 10.6 %copy-start = (f32[3,6,6]{2,1,0:T(8,128)S(1)}, f32[3,6,6]{2,1,0:T(8,128)}, u32[]{:S(2)}) copy-start(f32[3,6,6]{2,1,0:T(8,128)} %refs_9_.2) | copy-start | bytes 1300
  36.4 10.6 %copy-start.1 = (s32[768]{0:T(1024)S(1)}, s32[768]{0:T(1024)}, u32[]{:S(2)}) copy-start(s32[768]{0:T(1024)} %param.18) | copy-start | bytes 9220
  36.4 10.6 %copy-start.2 = (s32[1,32,4]{1,2,0:T(4,128)S(1)}, s32[1,32,4]{1,2,0:T(4,128)}, u32[]{:S(2)}) copy-start(s32[1,32,4]{1,2,0:T(4,128)} %param.21) | copy-start | bytes 1540
  36.4 10.6 %copy-start.3 = (s32[1,32,1]{1,2,0:T(1,128)S(1)}, s32[1,32,1]{1,2,0:T(1,128)}, u32[]{:S(2)}) copy-start(s32[1,32,1]{1,2,0:T(1,128)} %param.20) | copy-start | bytes 388
  36.4 10.6 %copy-start.4 = (s32[128]{0:T(128)S(1)}, s32[128]{0:T(128)}, u32[]{:S(2)}) copy-start(s32[128]{0:T(128)} %param.17) | copy-start | bytes 1540
  36.5 10.6 %copy-start.5 = (f32[6]{0:T(128)S(1)}, f32[6]{0:T(128)}, u32[]{:S(2)}) copy-start(f32[6]{0:T(128)} %refs_10_.1) | copy-start | bytes 76
  36.5 10.6 %copy-start.6 = (bf16[512,512]{1,0:T(8,128)(2,1)S(1)}, bf16[512,512]{1,0:T(8,128)(2,1)}, u32[]{:S(2)}) copy-start(bf16[512,512]{1,0:T(8,128)(2,1)} %constant.22.clone.refs_13_) | copy-start | bytes 1572868
  36.5 10.6 %copy-start.7 = (f32[128,512]{1,0:T(8,128)S(1)}, f32[128,512]{1,0:T(8,128)}, u32[]{:S(2)}) copy-start(f32[128,512]{1,0:T(8,128)} %constant.23.clone.refs_5_) | copy-start | bytes 786436
